TPU v7x, 256 devices: a whole 4x4x8 slice. The times are simulated.
256 devices in a mesh: row: 8 (over x, core), col: 32 (over y, z).
Axes of the slice: x: 4, y: 4, z: 8, core: 2. Of those that a mesh axis runs over, the one named last changes fastest.
Arguments:
- kernel: float32 [16384, 16384], P('row', 'col'), may hold values from 0 to 9, as said below
Outputs:
- factored: float32 [16384, 16384], P('row', 'col')
Inputs may be any that keep to these rules, and one draw needn't show every extreme that they name: `kernel`: ordered is symmetric and equals a positive semi-definite matrix plus a diagonal whose entries are 0.5 or more.
All inputs are finite; a program needn't handle non-finite values.
Results may differ from a plain program's by a relative error of at most 0.0003.
Values sent between devices are 32-bit elements; how exact they have to be, the bound alone decides.
No kernel may reach another device: no remote copies, remote signals or barrier semaphores. Data moves between devices by JAX's collectives and lax.ppermute only.
A program may use at most 128 MiB of HBM per device.

v0:
```python
import jax
import jax.numpy as jnp
from jax import lax
from jax.experimental import pallas as pl
from jax.experimental.pallas import tpu as pltpu
from jax.sharding import Mesh
from jax.sharding import PartitionSpec as P

NB = 256
PANELS = 3
LEAD = NB * PANELS
HALF = 128
F32 = jnp.float32
BF16 = jnp.bfloat16


def split(value):
    high = value.astype(BF16)
    return high, (value - high.astype(F32)).astype(BF16)


def dot_split(left, right, left_dim, right_dim):
    left_high, left_low = split(left)
    right_high, right_low = split(right)

    def dot(a, b):
        return lax.dot_general(a, b, (((left_dim,), (right_dim,)), ((), ())), preferred_element_type=F32)

    return dot(left_low, right_high) + dot(left_high, right_low) + dot(left_high, right_high)


def row_of(value, step):
    return jnp.broadcast_to(value[step : step + 1], value.shape)


def inverse_factor(block):
    groups = HALF // 8
    rows = lax.broadcasted_iota(jnp.int32, (8, HALF), 0)
    lanes = lax.broadcasted_iota(jnp.int32, (8, HALF), 1)
    left = [block[8 * g : 8 * g + 8] for g in range(groups)]
    right = [(lanes == rows + 8 * g).astype(F32) for g in range(groups)]
    for first in range(groups):
        columns = [
            [
                jnp.broadcast_to(left[g][:, 8 * first + j : 8 * first + j + 1], (8, HALF))
                if g >= first
                else None
                for g in range(groups)
            ]
            for j in range(8)
        ]
        pivots = rows.astype(F32)
        for j in range(8):
            pivot = row_of(columns[j][first], j)
            inverse = pl.reciprocal(pivot, approx=True)
            inverse = inverse * (2.0 - pivot * inverse)
            pivots = jnp.where(rows == j, pivot, pivots)
            left_row = row_of(left[first], j)
            right_row = row_of(right[first], j)
            heads = [row_of(columns[i][first], j) for i in range(j + 1, 8)]
            for g in range(first, groups):
                scale = columns[j][g] * inverse
                if g == first:
                    if j == 7:
                        continue
                    scale = jnp.where(rows > j, scale, 0.0)
                for i in range(j + 1, 8):
                    columns[i][g] = columns[i][g] - scale * heads[i - j - 1]
                left[g] = left[g] - scale * left_row
                right[g] = right[g] - scale * right_row
        right[first] = right[first] * lax.rsqrt(pivots)
    return jnp.concatenate(right, 0)


BLOCKS = [(k, j) for k in range(PANELS) for j in range(k + 1)]


def factor_kernel(lead_ref, work, inv):
    for slot, (k, j) in enumerate(BLOCKS):
        for r in range(8):
            at = k * NB + r * PIECE
            work[at : at + PIECE, j * NB : (j + 1) * NB] = lead_ref[r, slot]

    @pl.loop(0, 2 * PANELS)
    def _(p):
        at = pl.multiple_of(p * HALF, HALF)
        inverse = inverse_factor(work[pl.ds(at, HALF), pl.ds(at, HALF)])

        @pl.when(p % 2 == 0)
        def _():
            inv[pl.ds(at, HALF), 0:HALF] = inverse
            inv[pl.ds(at, HALF), HALF:NB] = jnp.zeros_like(inverse)

        @pl.when(p % 2 == 1)
        def _():
            before = pl.multiple_of((p - 1) * HALF, HALF)
            cross = dot_split(work[pl.ds(at, HALF), pl.ds(before, HALF)], inv[pl.ds(before, HALF), 0:HALF], 1, 0)
            inv[pl.ds(at, HALF), 0:HALF] = -dot_split(inverse, cross, 1, 0)
            inv[pl.ds(at, HALF), HALF:NB] = inverse

        for done in range(2 * PANELS - 1):

            @pl.when(p == done)
            def _():
                here = slice(done * HALF, (done + 1) * HALF)
                below = slice((done + 1) * HALF, LEAD)
                factor = dot_split(work[below, here], inverse, 1, 1)
                work[below, here] = factor
                work[below, below] = work[below, below] - dot_split(factor, factor, 1, 1)


def factor_lead(lead):
    vmem = pl.BlockSpec(memory_space=pltpu.VMEM)
    return pl.pallas_call(
        factor_kernel,
        out_shape=[jax.ShapeDtypeStruct((LEAD, LEAD), F32), jax.ShapeDtypeStruct((LEAD, NB), F32)],
        in_specs=[vmem],
        out_specs=[vmem, vmem],
        compiler_params=pltpu.CompilerParams(vmem_limit_bytes=24 * 2**20),
        cost_estimate=pl.CostEstimate(flops=20 * 10**9, bytes_accessed=6 * 2**20, transcendentals=0),
        name="factor_lead",
    )(lead)


def solve_kernel(place_ref, work, inv, cols_ref, high_ref, low_ref, rhs):
    my_col = place_ref[1]
    rhs[...] = cols_ref[...]
    for p in range(PANELS):
        here = slice(p * NB, (p + 1) * NB)
        rhs[here] = dot_split(inv[here], rhs[here], 1, 0)
        if p + 1 < PANELS:
            below = slice((p + 1) * NB, LEAD)
            rhs[below] = rhs[below] - dot_split(work[below, here], rhs[here], 1, 0)

    @pl.when(my_col < PANELS)
    def _():
        rows = lax.broadcasted_iota(jnp.int32, (LEAD, NB), 0)
        lanes = lax.broadcasted_iota(jnp.int32, (LEAD, NB), 1)
        rhs[:, 0:NB] = (rows == lanes + my_col * NB).astype(F32)

    for p in reversed(range(PANELS)):
        here = slice(p * NB, (p + 1) * NB)
        solved = dot_split(inv[here].T, rhs[here], 1, 0)
        rhs[here] = solved
        if p > 0:
            above = slice(0, p * NB)
            rhs[above] = rhs[above] - dot_split(work[here, above].T, solved, 1, 0)
    high, low = split(rhs[...])
    high_ref[...] = high
    low_ref[...] = low


def solve_lead(place, work, inv, cols):
    width = cols.shape[1]
    vmem = pl.BlockSpec(memory_space=pltpu.VMEM)
    return pl.pallas_call(
        solve_kernel,
        out_shape=[jax.ShapeDtypeStruct((LEAD, width), BF16)] * 2,
        in_specs=[pl.BlockSpec(memory_space=pltpu.SMEM), vmem, vmem, vmem],
        out_specs=[vmem, vmem],
        scratch_shapes=[pltpu.VMEM((LEAD, width), F32)],
        compiler_params=pltpu.CompilerParams(vmem_limit_bytes=24 * 2**20),
        cost_estimate=pl.CostEstimate(flops=8 * 10**9, bytes_accessed=6 * 2**20, transcendentals=0),
        name="solve_lead",
    )(place, work, inv, cols)


def update_kernel(place_ref, base_ref, rows_ref, high_ref, low_ref, out_ref):
    first_id = place_ref[0] + place_ref[2] * pl.program_id(0)
    near = place_ref[1]
    left = slice(0, NB)
    right = slice(NB, 2 * NB)
    panel = near < PANELS

    def product(rows, span):
        parts = [split(rows_ref[0, rows, k].reshape(-1, NB)) for k in range(PANELS)]
        high = jnp.concatenate([part[0] for part in parts], axis=1)
        low = jnp.concatenate([part[1] for part in parts], axis=1)
        total = jnp.dot(low, high_ref[:, span], preferred_element_type=F32)
        total = total + jnp.dot(high, low_ref[:, span], preferred_element_type=F32)
        return total + jnp.dot(high, high_ref[:, span], preferred_element_type=F32)

    @pl.when(first_id >= near)
    def _():
        total = product(slice(0, 8), left).reshape(2, NB, NB)

        @pl.when(panel)
        def _():
            rows = lax.broadcasted_iota(jnp.int32, (NB, NB), 0)
            lanes = lax.broadcasted_iota(jnp.int32, (NB, NB), 1)
            out_ref[0, :, left] = jnp.where((rows >= lanes) | (first_id > near), total[0], 0.0)
            out_ref[1, :, left] = total[1]

        @pl.when(jnp.logical_not(panel))
        def _():
            out_ref[:, :, left] = base_ref[:, :, left] - total

        out_ref[0, :, right] = jnp.zeros((NB, NB), F32)
        out_ref[1, :, right] = base_ref[1, :, right] - product(slice(4, 8), right)

    @pl.when(first_id < near)
    def _():
        out_ref[0] = jnp.zeros((NB, 2 * NB), F32)
        total = product(slice(4, 8), left)
        out_ref[1, :, left] = jnp.where(panel, total, base_ref[1, :, left] - total)
        out_ref[1, :, right] = jnp.zeros((NB, NB), F32)


def update(place, base, gathered, high, low):
    rows, width = base.shape
    pairs = base.reshape(2, rows // 2, width)
    return pl.pallas_call(
        update_kernel,
        grid=(rows // NB // 2,),
        out_shape=jax.ShapeDtypeStruct(pairs.shape, F32),
        in_specs=[
            pl.BlockSpec(memory_space=pltpu.SMEM),
            pl.BlockSpec((2, NB, width), lambda y: (0, y, 0)),
            pl.BlockSpec((1, 8, PANELS, 64, NB), lambda y: (y, 0, 0, 0, 0)),
            pl.BlockSpec(memory_space=pltpu.VMEM),
            pl.BlockSpec(memory_space=pltpu.VMEM),
        ],
        out_specs=pl.BlockSpec((2, NB, width), lambda y: (0, y, 0)),
        compiler_params=pltpu.CompilerParams(vmem_limit_bytes=57 * 2**20),
        cost_estimate=pl.CostEstimate(flops=5 * 10**9, bytes_accessed=16 * 2**20, transcendentals=0),
        name="update",
    )(place, pairs, gathered, high, low).reshape(rows, width)


N_X, N_CORE, N_Y, N_Z = 4, 2, 4, 8
N_ROW = N_X * N_CORE
N_COL = N_Y * N_Z
AXES = ("x", "core", "y", "z")
PIECE = NB // N_Z


def device(row, y, z):
    return (row * N_Y + y) * N_Z + z


def send(value, pairs):
    return lax.ppermute(value, AXES, pairs)


def pick(stacked, index):
    return lax.dynamic_index_in_dim(stacked, index % stacked.shape[0], 0, keepdims=False)


def scatter_rows(strip, my_row, my_y, my_z):
    pieces = strip.T.reshape(N_Z, 2 * NB // N_Z, NB)
    received = []
    for step in range(N_Z):
        pairs = [
            (device(k, y, z), device(z, y, (z + step + k) % N_Z))
            for k in range(PANELS)
            for y in range(N_Y)
            for z in range(N_Z)
        ]
        received.append(send(pick(pieces, my_z + step + my_row), pairs))
    received = jnp.stack(received)
    return jnp.stack([pick(received, my_z - my_row - k) for k in range(PANELS)])


def scatter_lead(strip, my_x, my_core):
    pieces = strip[:, 0:NB].reshape(N_X, N_CORE, PIECE, NB)
    keep = lax.dynamic_index_in_dim(pieces, my_core, 1, keepdims=False)
    give = lax.dynamic_index_in_dim(pieces, 1 - my_core, 1, keepdims=False)
    got = lax.ppermute(give, "core", [(0, 1), (1, 0)])
    both = jnp.stack(
        [jnp.where(my_core == 0, keep, got), jnp.where(my_core == 0, got, keep)], axis=1
    )
    received = [pick(both, my_x)]
    for step in range(1, N_X):
        pairs = [
            (device(N_CORE * x + core, 0, j), device(N_CORE * ((x + step) % N_X) + core, 0, j))
            for x in range(2)
            for core in range(N_CORE)
            for j in range(PANELS)
        ]
        received.append(send(pick(both, my_x + step), pairs))
    received = jnp.stack(received)
    return jnp.concatenate([pick(received, my_x), pick(received, my_x - 1)[0:1]], axis=0)


def spread_lead(parts, my_z):
    far = send(
        parts, [(device(r, 0, j), device(r, 0, j + N_Z // 2)) for r in range(N_ROW) for j in range(PANELS)]
    )
    hold = jnp.where(my_z >= N_Z // 2, far, parts)
    received = [hold]
    for step in range(1, N_Z // 2):
        pairs = [
            (device(r, 0, j + half), device(r, 0, (j + half + step) % N_Z))
            for r in range(N_ROW)
            for j in range(PANELS)
            for half in (0, N_Z // 2)
        ]
        received.append(send(hold, pairs))
    received = jnp.stack(received)
    spread = [pick(received, my_z - j) for j in range(PANELS)]
    return jnp.stack([spread[j][k] for k, j in BLOCKS])


def share_lead(mine, my_x, my_y):
    others = [
        send(mine, [(device(r, 0, z), device(r, y, z)) for r in range(N_ROW) for z in range(N_Z)])
        for y in range(1, N_Y)
    ]
    mine = jnp.where(my_y == 0, mine, others[0] + others[1] + others[2])
    around = [mine] + [
        lax.ppermute(mine, "x", [(x, (x + step) % N_X) for x in range(N_X)]) for step in range(1, N_X)
    ]
    around = jnp.stack(around)
    return jnp.stack([pick(around, my_x - x) for x in range(N_X)])


def swap_lead(half, my_core):
    other = lax.ppermute(half, "core", [(0, 1), (1, 0)])
    first = jnp.where(my_core == 0, half, other)
    second = jnp.where(my_core == 0, other, half)
    return jnp.stack([first, second], axis=1).reshape(N_ROW, len(BLOCKS), PIECE, NB)


def col_pairs(moves):
    return [
        (device(2 * a + core, y, z), device(2 * b + core, y, z))
        for a, b, cores in moves
        for core in range(cores)
        for y in range(N_Y)
        for z in range(N_Z)
    ]


def cols_out(strip):
    return send(strip, col_pairs([(0, 1, 2), (1, 2, 1)])), send(strip, col_pairs([(0, 3, 2), (1, 0, 1)]))


def cols_on(up):
    return send(up, col_pairs([(1, 2, 2), (2, 3, 1)]))


def swap_cols(strip, up, down, onward, my_x, my_core):
    own = jnp.where(my_x == 0, strip, jnp.where(my_x == 1, up, jnp.where(my_x == 2, onward, down)))
    last = jnp.where(my_x == 0, down, jnp.where(my_x == 1, strip, jnp.where(my_x == 2, up, onward)))
    other = lax.ppermute(own, "core", [(0, 1), (1, 0)])
    passed = lax.ppermute(last, "core", [(0, 1)])
    first = jnp.where(my_core == 0, own, other)
    second = jnp.where(my_core == 0, other, own)
    last = jnp.where(my_core == 0, last, passed)
    return jnp.concatenate([first, second, last], axis=0)


def body(kernel):
    my_x, my_core = lax.axis_index("x"), lax.axis_index("core")
    my_y, my_z = lax.axis_index("y"), lax.axis_index("z")
    my_row = my_x * N_CORE + my_core
    my_col = my_y * N_Z + my_z
    place = jnp.stack([my_row, my_col, jnp.int32(N_ROW), jnp.int32(N_COL)]).astype(jnp.int32)
    strip = kernel[0:NB]
    parts = scatter_lead(strip, my_x, my_core)
    strip, parts = lax.optimization_barrier((strip, parts))
    mine = scatter_rows(strip, my_row, my_y, my_z)
    eighth = spread_lead(parts, my_z)
    strip, mine = lax.optimization_barrier((strip, mine))
    gathered = lax.all_gather(mine, ("y", "z")).reshape(N_Y, N_Z, PANELS, 2 * NB // N_Z, NB)
    up, down = cols_out(strip)
    eighth, up, down = lax.optimization_barrier((eighth, up, down))
    onward = cols_on(up)
    quarter = share_lead(eighth, my_x, my_y)
    quarter, onward = lax.optimization_barrier((quarter, onward))
    lead = swap_lead(quarter, my_core)
    cols = swap_cols(strip, up, down, onward, my_x, my_core)
    work, inv = factor_lead(lead)
    high, low = solve_lead(place, work, inv, cols)
    return update(place, kernel, gathered, high, low)


def solution(mesh):
    fine = Mesh(mesh.devices.reshape(N_X, N_CORE, N_Y, N_Z), AXES)
    placed = P(("x", "core"), ("y", "z"))
    return jax.shard_map(body, mesh=fine, in_specs=(placed,), out_specs=placed, check_vma=False)
```

profile of v0, /device:TPU:21, one launch (start us, length us, event | category | flops | bytes accessed | tf_op | source)
XLA Modules:
  0.0 167.1 jit_solution(8457926058835351800)
XLA Ops:
  6.5 1.0 slice.50
  7.5 0.8 collective-permute-start
  8.3 1.0 collective-permute-done
  9.3 0.7 collective-permute-start.1
  10.0 0.7 collective-permute-start.2
  10.7 0.7 collective-permute-start.3
  11.4 1.1 slice.49
  12.6 0.0 collective-permute-done.1
  12.6 0.0 collective-permute-done.2
  12.7 0.2 copy.16
  12.9 0.1 dynamic-slice_bitcast_fusion.1
  13.0 0.7 collective-permute-start.4
  13.7 1.3 collective-permute-start.5
  15.0 1.3 collective-permute-start.6
  16.3 1.3 collective-permute-start.7
  17.6 0.7 collective-permute-start.8
  18.3 0.0 collective-permute-done.4
  18.3 0.7 collective-permute-start.9
  19.0 10.2 %collective-permute-done.5 = f32[64,256]{1,0:T(8,128)S(1)} collective-permute-done((f32[64,256]{1,0:T(8,128)S(1)}, f32[64,256]{1,0:T(8,128)S(1)}, u32[]{:S(2)}, u32[]{:S(2)}) %collective-permute-start.5) | collective-permute-done | bytes 65568 | tf_op jit(solution)/shard_map/ppermute | solution.py:242
  29.2 0.7 collective-permute-start.10
  29.8 4.4 %collective-permute-done.6 = f32[64,256]{1,0:T(8,128)S(1)} collective-permute-done((f32[64,256]{1,0:T(8,128)S(1)}, f32[64,256]{1,0:T(8,128)S(1)}, u32[]{:S(2)}, u32[]{:S(2)}) %collective-permute-start.6) | collective-permute-done | bytes 65568 | tf_op jit(solution)/shard_map/ppermute | solution.py:242
  34.2 0.7 collective-permute-start.11
  34.9 2.5 %collective-permute-done.7 = f32[64,256]{1,0:T(8,128)S(1)} collective-permute-done((f32[64,256]{1,0:T(8,128)S(1)}, f32[64,256]{1,0:T(8,128)S(1)}, u32[]{:S(2)}, u32[]{:S(2)}) %collective-permute-start.7) | collective-permute-done | bytes 65568 | tf_op jit(solution)/shard_map/ppermute | solution.py:242
  37.5 0.7 pad_maximum_fusion.6
  38.2 0.0 all-gather.3.cloned.1.call-update
  38.2 0.7 collective-permute-start.12
  39.0 0.7 collective-permute-start.13
  39.6 0.7 collective-permute-start.14
  40.3 0.7 collective-permute-start.15
  41.0 0.7 collective-permute-start.16
  41.7 0.7 collective-permute-start.17
  42.7 0.7 collective-permute-start.18
  43.3 1.3 collective-permute-start.19
  44.6 0.7 collective-permute-start.20
  45.3 35.5 %collective-permute-done.19 = f32[6,32,256]{2,1,0:T(8,128)S(1)} collective-permute-done((f32[6,32,256]{2,1,0:T(8,128)S(1)}, f32[6,32,256]{2,1,0:T(8,128)S(1)}, u32[]{:S(2)}, u32[]{:S(2)}) %collective-permute-start.19) | collective-permute-done | bytes 196640 | tf_op jit(solution)/shard_map/ppermute | solution.py:242
  80.8 0.1 add_select_fusion
  80.8 1.2 collective-permute-start.21
  82.0 1.3 collective-permute-start.23
  83.3 1.3 collective-permute-start.24
  84.7 0.8 collective-permute-done.21
  85.4 4.8 %collective-permute-done.22 = f32[6,32,256]{2,1,0:T(8,128)S(1)} collective-permute-done((f32[6,32,256]{2,1,0:T(8,128)S(1)}, f32[6,32,256]{2,1,0:T(8,128)S(1)}, u32[]{:S(2)}, u32[]{:S(2)}) %collective-permute-start.22) | collective-permute-done | bytes 196640 | tf_op jit(solution)/shard_map/ppermute | solution.py:311
  90.2 0.8 collective-permute-done.23
  91.0 0.1 pad_maximum_fusion.2
  91.0 0.1 constant_dynamic-slice_fusion.3
  91.1 0.1 pad_maximum_fusion.3
  91.2 11.5 %collective-permute-done.24 = f32[256,512]{1,0:T(8,128)} collective-permute-done((f32[256,512]{1,0:T(8,128)S(1)}, f32[256,512]{1,0:T(8,128)}, u32[]{:S(2)}, u32[]{:S(2)}) %collective-permute-start.24) | collective-permute-done | bytes 524320 | tf_op jit(solution)/shard_map/ppermute | solution.py:242
  102.7 1.3 select_select_fusion.1
  104.0 1.3 collective-permute-start.27
  105.3 1.7 %collective-permute-start.26 = (f32[256,512]{1,0:T(8,128)S(1)}, f32[256,512]{1,0:T(8,128)S(1)}, u32[]{:S(2)}, u32[]{:S(2)}) collective-permute-start(f32[256,512]{1,0:T(8,128)S(1)} %get-tuple-element.31), channel_id=1, source_target_pairs={{0,32},{32,0},{1,33},{33,1},{2,34},{34,2},{3,35},{35,3},{4,36},{36... | collective-permute-start | bytes 1572872 | tf_op jit(solution)/shard_map/ppermute | solution.py:345
  107.0 0.3 collective-permute-start.25
  107.3 0.1 pad_add_fusion.place_ref
  107.4 0.9 collective-permute-done.27
  108.3 0.1 broadcast_select_fusion
  108.4 0.7 collective-permute-done.26
  109.0 0.1 broadcast_select_fusion.2
  109.1 0.1 pad_maximum_fusion.1.cols_ref
  109.3 0.9 collective-permute-done.25
  110.2 0.2 select_bitcast_fusion.1
  110.3 0.1 pad_maximum_fusion
  110.4 33.4 %factor_lead.1 = (f32[768,768]{1,0:T(8,128)S(1)}, f32[768,256]{1,0:T(8,128)S(1)}) custom-call(f32[8,6,32,256]{3,2,1,0:T(8,128)S(1)} %bitcast.107), custom_call_target="tpu_custom_call" | custom-call | flops 20000000000 | bytes 6291456 | tf_op jit(solution)/shard_map/factor_lead/pallas_call | solution.py:114
  143.8 4.5 %solve_lead.1 = (bf16[768,512]{1,0:T(8,128)(2,1)S(1)}, bf16[768,512]{1,0:T(8,128)(2,1)S(1)}) custom-call(s32[4]{0:T(128)S(1)} %pad_add_fusion.place_ref, f32[768,768]{1,0:T(8,128)S(1)} %get-tuple-element.25.work, f32[768,256]{1,0:T(8,128)S(1)} %get-tuple-element.26.inv, f32[768,512]{1,0:T(8,128)S(1)} %pad_maximum_fusion.1.cols_ref), custom_call_target="tpu_custom_call" | custom-call | flops 8000000000 | bytes 6291456 | tf_op jit(solution)/shard_map/solve_lead/pallas_call | solution.py:156
  148.4 0.9 copy-done.1
  149.3 0.9 copy-done.2
  150.2 10.0 %update.1 = f32[2,1024,512]{2,1,0:T(8,128)} custom-call(s32[4]{0:T(128)} %copy-done, f32[2,1024,512]{2,1,0:T(8,128)} %bitcast.117, f32[4,8,3,64,256]{4,3,2,1,0:T(8,128)} %bitcast.124, bf16[768,512]{1,0:T(8,128)(2,1)} %copy-done.1, bf16[768,512]{1,0:T(8,128)(2,1)} %copy-done.2), custom_call_target="tpu_custom_call" | custom-call | flops 5000000000 | bytes 16777216 | tf_op jit(solution)/shard_map/update/pallas_call | solution.py:212
  (44 shorter events, 0.4 us)
Async XLA Ops:
  6.5 143.7 %all-gather.3.cloned.1.call-start = ((), (), s32[]{:S(2)}) async-start(), calls=%async_computation | async-start | bytes 6488064 | tf_op jit(solution)/shard_map/all_gather | solution.py:365
  7.5 1.7 %collective-permute-start = (f32[4,32,256]{2,1,0:T(8,128)S(1)}, f32[4,32,256]{2,1,0:T(8,128)S(1)}, u32[]{:S(2)}, u32[]{:S(2)}) collective-permute-start(f32[4,32,256]{2,1,0:T(8,128)S(1)} %dynamic-slice_bitcast_fusion), channel_id=1, source_target_pairs={{0,32},{32,0},{1,33},{33,1},{2,34},{34,2},{3,35},{35,3},{4,36},{36... | collective-permute-start | bytes 393224 | tf_op jit(solution)/shard_map/ppermute | solution.py:268
  9.3 3.3 %collective-permute-start.1 = (f32[2,32,256]{2,1,0:T(8,128)S(1)}, f32[2,32,256]{2,1,0:T(8,128)S(1)}, u32[]{:S(2)}, u32[]{:S(2)}) collective-permute-start(f32[2,32,256]{2,1,0:T(8,128)S(1)} %get-tuple-element.55), channel_id=1, source_target_pairs={{0,64},{1,65},{2,66},{32,96},{33,97},{34,98},{64,128},{65,129},{66... | collective-permute-start | bytes 196616 | tf_op jit(solution)/shard_map/ppermute | solution.py:242
  10.0 2.6 %collective-permute-start.2 = (f32[2,32,256]{2,1,0:T(8,128)S(1)}, f32[2,32,256]{2,1,0:T(8,128)S(1)}, u32[]{:S(2)}, u32[]{:S(2)}) collective-permute-start(f32[2,32,256]{2,1,0:T(8,128)S(1)} %get-tuple-element.56), channel_id=1, source_target_pairs={{0,128},{1,129},{2,130},{32,160},{33,161},{34,162},{64,192},{65,19... | collective-permute-start | bytes 196616 | tf_op jit(solution)/shard_map/ppermute | solution.py:242
  10.7 1.9 %collective-permute-start.3 = (f32[2,32,256]{2,1,0:T(8,128)S(1)}, f32[2,32,256]{2,1,0:T(8,128)S(1)}, u32[]{:S(2)}, u32[]{:S(2)}) collective-permute-start(f32[2,32,256]{2,1,0:T(8,128)S(1)} %get-tuple-element.57), channel_id=1, source_target_pairs={{0,192},{1,193},{2,194},{32,224},{33,225},{34,226},{64,0},{65,1},{... | collective-permute-start | bytes 196616 | tf_op jit(solution)/shard_map/ppermute | solution.py:242
  13.0 5.3 %collective-permute-start.4 = (f32[64,256]{1,0:T(8,128)S(1)}, f32[64,256]{1,0:T(8,128)S(1)}, u32[]{:S(2)}, u32[]{:S(2)}) collective-permute-start(f32[64,256]{1,0:T(8,128)S(1)} %get-tuple-element.51), channel_id=1, source_target_pairs={{0,0},{1,33},{2,66},{3,99},{4,132},{5,165},{6,198},{7,231},{8,8},{... | collective-permute-start | bytes 196616 | tf_op jit(solution)/shard_map/ppermute | solution.py:242
  13.7 15.4 %collective-permute-start.5 = (f32[64,256]{1,0:T(8,128)S(1)}, f32[64,256]{1,0:T(8,128)S(1)}, u32[]{:S(2)}, u32[]{:S(2)}) collective-permute-start(f32[64,256]{1,0:T(8,128)S(1)} %get-tuple-element.50), channel_id=1, source_target_pairs={{0,1},{1,34},{2,67},{3,100},{4,133},{5,166},{6,199},{7,224},{8,9},... | collective-permute-start | bytes 196616 | tf_op jit(solution)/shard_map/ppermute | solution.py:242
  15.0 19.2 %collective-permute-start.6 = (f32[64,256]{1,0:T(8,128)S(1)}, f32[64,256]{1,0:T(8,128)S(1)}, u32[]{:S(2)}, u32[]{:S(2)}) collective-permute-start(f32[64,256]{1,0:T(8,128)S(1)} %get-tuple-element.49), channel_id=1, source_target_pairs={{0,2},{1,35},{2,68},{3,101},{4,134},{5,167},{6,192},{7,225},{8,10}... | collective-permute-start | bytes 196616 | tf_op jit(solution)/shard_map/ppermute | solution.py:242
  16.3 21.1 %collective-permute-start.7 = (f32[64,256]{1,0:T(8,128)S(1)}, f32[64,256]{1,0:T(8,128)S(1)}, u32[]{:S(2)}, u32[]{:S(2)}) collective-permute-start(f32[64,256]{1,0:T(8,128)S(1)} %get-tuple-element.48), channel_id=1, source_target_pairs={{0,3},{1,36},{2,69},{3,102},{4,135},{5,160},{6,193},{7,226},{8,11}... | collective-permute-start | bytes 196616 | tf_op jit(solution)/shard_map/ppermute | solution.py:242
  17.6 19.8 %collective-permute-start.8 = (f32[64,256]{1,0:T(8,128)S(1)}, f32[64,256]{1,0:T(8,128)S(1)}, u32[]{:S(2)}, u32[]{:S(2)}) collective-permute-start(f32[64,256]{1,0:T(8,128)S(1)} %get-tuple-element.47), channel_id=1, source_target_pairs={{0,4},{1,37},{2,70},{3,103},{4,128},{5,161},{6,194},{7,227},{8,12}... | collective-permute-start | bytes 196616 | tf_op jit(solution)/shard_map/ppermute | solution.py:242
  18.3 19.1 %collective-permute-start.9 = (f32[64,256]{1,0:T(8,128)S(1)}, f32[64,256]{1,0:T(8,128)S(1)}, u32[]{:S(2)}, u32[]{:S(2)}) collective-permute-start(f32[64,256]{1,0:T(8,128)S(1)} %get-tuple-element.46), channel_id=1, source_target_pairs={{0,5},{1,38},{2,71},{3,96},{4,129},{5,162},{6,195},{7,228},{8,13},... | collective-permute-start | bytes 196616 | tf_op jit(solution)/shard_map/ppermute | solution.py:242
  29.2 8.3 %collective-permute-start.10 = (f32[64,256]{1,0:T(8,128)S(1)}, f32[64,256]{1,0:T(8,128)S(1)}, u32[]{:S(2)}, u32[]{:S(2)}) collective-permute-start(f32[64,256]{1,0:T(8,128)S(1)} %get-tuple-element.45), channel_id=1, source_target_pairs={{0,6},{1,39},{2,64},{3,97},{4,130},{5,163},{6,196},{7,229},{8,14},... | collective-permute-start | bytes 196616 | tf_op jit(solution)/shard_map/ppermute | solution.py:242
  34.2 3.2 %collective-permute-start.11 = (f32[64,256]{1,0:T(8,128)S(1)}, f32[64,256]{1,0:T(8,128)S(1)}, u32[]{:S(2)}, u32[]{:S(2)}) collective-permute-start(f32[64,256]{1,0:T(8,128)S(1)} %get-tuple-element.44), channel_id=1, source_target_pairs={{0,7},{1,32},{2,65},{3,98},{4,131},{5,164},{6,197},{7,230},{8,15},... | collective-permute-start | bytes 196616 | tf_op jit(solution)/shard_map/ppermute | solution.py:242
  38.2 0.7 collective-permute-start.12
  39.0 3.5 %collective-permute-start.13 = (f32[3,32,256]{2,1,0:T(8,128)S(1)}, f32[3,32,256]{2,1,0:T(8,128)S(1)}, u32[]{:S(2)}, u32[]{:S(2)}) collective-permute-start(f32[3,32,256]{2,1,0:T(8,128)S(1)} %broadcast_select_fusion.3), channel_id=1, source_target_pairs={{0,1},{4,5},{1,2},{5,6},{2,3},{6,7},{32,33},{36,37},{33,34},{37,38... | collective-permute-start | bytes 294920 | tf_op jit(solution)/shard_map/ppermute | solution.py:242
  39.6 2.8 %collective-permute-start.14 = (f32[3,32,256]{2,1,0:T(8,128)S(1)}, f32[3,32,256]{2,1,0:T(8,128)S(1)}, u32[]{:S(2)}, u32[]{:S(2)}) collective-permute-start(f32[3,32,256]{2,1,0:T(8,128)S(1)} %broadcast_select_fusion.3), channel_id=1, source_target_pairs={{0,2},{4,6},{1,3},{5,7},{2,4},{6,0},{32,34},{36,38},{33,35},{37,39... | collective-permute-start | bytes 294920 | tf_op jit(solution)/shard_map/ppermute | solution.py:242
  40.3 2.2 %collective-permute-start.15 = (f32[3,32,256]{2,1,0:T(8,128)S(1)}, f32[3,32,256]{2,1,0:T(8,128)S(1)}, u32[]{:S(2)}, u32[]{:S(2)}) collective-permute-start(f32[3,32,256]{2,1,0:T(8,128)S(1)} %broadcast_select_fusion.3), channel_id=1, source_target_pairs={{0,3},{4,7},{1,4},{5,0},{2,5},{6,1},{32,35},{36,39},{33,36},{37,32... | collective-permute-start | bytes 294920 | tf_op jit(solution)/shard_map/ppermute | solution.py:242
  41.0 1.6 collective-permute-start.16
  41.7 0.9 collective-permute-start.17
  42.7 2.7 %collective-permute-start.18 = (f32[6,32,256]{2,1,0:T(8,128)S(1)}, f32[6,32,256]{2,1,0:T(8,128)S(1)}, u32[]{:S(2)}, u32[]{:S(2)}) collective-permute-start(f32[6,32,256]{2,1,0:T(8,128)S(1)} %fusion.9), channel_id=1, source_target_pairs={{0,8},{1,9},{2,10},{3,11},{4,12},{5,13},{6,14},{7,15},{32,40},{33,... | collective-permute-start | bytes 589832 | tf_op jit(solution)/shard_map/ppermute | solution.py:242
  43.3 37.4 %collective-permute-start.19 = (f32[6,32,256]{2,1,0:T(8,128)S(1)}, f32[6,32,256]{2,1,0:T(8,128)S(1)}, u32[]{:S(2)}, u32[]{:S(2)}) collective-permute-start(f32[6,32,256]{2,1,0:T(8,128)S(1)} %fusion.9), channel_id=1, source_target_pairs={{0,16},{1,17},{2,18},{3,19},{4,20},{5,21},{6,22},{7,23},{32,48},{3... | collective-permute-start | bytes 589832 | tf_op jit(solution)/shard_map/ppermute | solution.py:242
  44.6 36.2 %collective-permute-start.20 = (f32[6,32,256]{2,1,0:T(8,128)S(1)}, f32[6,32,256]{2,1,0:T(8,128)S(1)}, u32[]{:S(2)}, u32[]{:S(2)}) collective-permute-start(f32[6,32,256]{2,1,0:T(8,128)S(1)} %fusion.9), channel_id=1, source_target_pairs={{0,24},{1,25},{2,26},{3,27},{4,28},{5,29},{6,30},{7,31},{32,56},{3... | collective-permute-start | bytes 589832 | tf_op jit(solution)/shard_map/ppermute | solution.py:242
  80.8 4.6 %collective-permute-start.21 = (f32[6,32,256]{2,1,0:T(8,128)S(1)}, f32[6,32,256]{2,1,0:T(8,128)S(1)}, u32[]{:S(2)}, u32[]{:S(2)}) collective-permute-start(f32[6,32,256]{2,1,0:T(8,128)S(1)} %add_select_fusion), channel_id=1, source_target_pairs={{0,64},{64,128},{128,192},{192,0},{1,65},{65,129},{129,193},{193,1... | collective-permute-start | bytes 589832 | tf_op jit(solution)/shard_map/ppermute | solution.py:311
  82.0 8.2 %collective-permute-start.22 = (f32[6,32,256]{2,1,0:T(8,128)S(1)}, f32[6,32,256]{2,1,0:T(8,128)S(1)}, u32[]{:S(2)}, u32[]{:S(2)}) collective-permute-start(f32[6,32,256]{2,1,0:T(8,128)S(1)} %add_select_fusion), channel_id=1, source_target_pairs={{0,128},{64,192},{128,0},{192,64},{1,129},{65,193},{129,1},{193,65... | collective-permute-start | bytes 589832 | tf_op jit(solution)/shard_map/ppermute | solution.py:311
  82.0 8.9 %collective-permute-start.23 = (f32[6,32,256]{2,1,0:T(8,128)S(1)}, f32[6,32,256]{2,1,0:T(8,128)S(1)}, u32[]{:S(2)}, u32[]{:S(2)}) collective-permute-start(f32[6,32,256]{2,1,0:T(8,128)S(1)} %add_select_fusion), channel_id=1, source_target_pairs={{0,192},{64,0},{128,64},{192,128},{1,193},{65,1},{129,65},{193,129... | collective-permute-start | bytes 589832 | tf_op jit(solution)/shard_map/ppermute | solution.py:311
  83.3 19.4 %collective-permute-start.24 = (f32[256,512]{1,0:T(8,128)S(1)}, f32[256,512]{1,0:T(8,128)}, u32[]{:S(2)}, u32[]{:S(2)}) collective-permute-start(f32[256,512]{1,0:T(8,128)S(1)} %collective-permute-done.16), channel_id=1, source_target_pairs={{64,128},{65,129},{66,130},{67,131},{68,132},{69,133},{70,134},{71... | collective-permute-start | bytes 1572872 | tf_op jit(solution)/shard_map/ppermute | solution.py:242
  104.0 4.3 %collective-permute-start.27 = (f32[256,512]{1,0:T(8,128)S(1)}, f32[256,512]{1,0:T(8,128)S(1)}, u32[]{:S(2)}, u32[]{:S(2)}) collective-permute-start(f32[256,512]{1,0:T(8,128)S(1)} %get-tuple-element.32), channel_id=1, source_target_pairs={{0,32},{1,33},{2,34},{3,35},{4,36},{5,37},{6,38},{7,39},{8,40},{9,... | collective-permute-start | bytes 1572872 | tf_op jit(solution)/shard_map/ppermute | solution.py:346
  105.3 3.7 %collective-permute-start.26 = (f32[256,512]{1,0:T(8,128)S(1)}, f32[256,512]{1,0:T(8,128)S(1)}, u32[]{:S(2)}, u32[]{:S(2)}) collective-permute-start(f32[256,512]{1,0:T(8,128)S(1)} %get-tuple-element.31), channel_id=1, source_target_pairs={{0,32},{32,0},{1,33},{33,1},{2,34},{34,2},{3,35},{35,3},{4,36},{36... | collective-permute-start | bytes 1572872 | tf_op jit(solution)/shard_map/ppermute | solution.py:345
  107.0 3.1 %collective-permute-start.25 = (f32[4,6,32,256]{3,2,1,0:T(8,128)S(1)}, f32[4,6,32,256]{3,2,1,0:T(8,128)S(1)}, u32[]{:S(2)}, u32[]{:S(2)}) collective-permute-start(f32[4,6,32,256]{3,2,1,0:T(8,128)S(1)} %pad_maximum_fusion.3), channel_id=1, source_target_pairs={{0,32},{32,0},{1,33},{33,1},{2,34},{34,2},{3,35},{35,3},{4,36},{36... | collective-permute-start | bytes 2359304 | tf_op jit(solution)/shard_map/ppermute | solution.py:318
  107.4 36.5 %copy-start = (s32[4]{0:T(128)}, s32[4]{0:T(128)S(1)}, u32[]{:S(2)}) copy-start(s32[4]{0:T(128)S(1)} %pad_add_fusion.place_ref) | copy-start | bytes 52
  148.4 0.9 copy-start.1
  149.3 0.9 copy-start.2
Sparse Core Ops, SparseCore 0:
  38.4 91.0 all-gather.2
where the time goes:
time: 170 us; the launch traced here: 167 us
  waiting for transfers between devices  73.8 us (43%)
  Pallas kernels  48 us (28%)
  starting transfers between devices  23.7 us (14%)
  between operations  14.3 us (8%)
  local copies, waits for them, and re-layouts  4.4 us (3%)
  other arithmetic  2.88 us (2%)
    ppermute x21, waiting for transfers between devices, send(): return lax.ppermute(value, AXES, pairs)  64 us
    pallas_call x1, Pallas kernels, factor_lead(): pl.pallas_call(factor_kernel, out_shape=[jax.ShapeDtypeStruct((LEAD, LEAD...  33.4 us
    ppermute x21, starting transfers between devices, send(): return lax.ppermute(value, AXES, pairs)  17.1 us
    pallas_call x1, Pallas kernels, update(): pl.pallas_call(update_kernel, grid=(rows // NB // 2,), out_shape=jax.Shap...  10 us
    ppermute x3, waiting for transfers between devices, share_lead(): lax.ppermute(mine, 'x', [(x, (x + step) % N_X) for x in range(N_X)])  6.33 us
    pallas_call x1, Pallas kernels, solve_lead(): pl.pallas_call(solve_kernel, out_shape=[jax.ShapeDtypeStruct((LEAD, width...  4.52 us
  transfers between devices with their start and end apart: 29, of which 12 were waited for; matrix products, arithmetic and copies ran while one was open for 2% of the time, Pallas kernels for 23%

commit v1 on v0

--- a/solution.py
+++ b/solution.py
@@ -30,7 +30,7 @@
 
 
 def row_of(value, step):
-    return jnp.broadcast_to(value[step : step + 1], value.shape)
+    return jnp.take_along_axis(value, jnp.full(value.shape, step, jnp.int32), axis=0)
 
 
 def inverse_factor(block):
@@ -72,14 +72,18 @@
     return jnp.concatenate(right, 0)
 
 
-BLOCKS = [(k, j) for k in range(PANELS) for j in range(k + 1)]
+BLOCKS = [(j, j) for j in range(PANELS)] + [((j + 1) % PANELS, j) for j in range(PANELS)]
 
 
 def factor_kernel(lead_ref, work, inv):
     for slot, (k, j) in enumerate(BLOCKS):
-        for r in range(8):
-            at = k * NB + r * PIECE
-            work[at : at + PIECE, j * NB : (j + 1) * NB] = lead_ref[r, slot]
+        if k >= j:
+            for r in range(8):
+                at = k * NB + r * PIECE
+                work[at : at + PIECE, j * NB : (j + 1) * NB] = lead_ref[r, slot]
+        else:
+            turned = lead_ref[:, slot].reshape(NB, NB).T
+            work[j * NB : (j + 1) * NB, k * NB : (k + 1) * NB] = turned
 
     @pl.loop(0, 2 * PANELS)
     def _(p):
@@ -176,9 +180,13 @@
         parts = [split(rows_ref[0, rows, k].reshape(-1, NB)) for k in range(PANELS)]
         high = jnp.concatenate([part[0] for part in parts], axis=1)
         low = jnp.concatenate([part[1] for part in parts], axis=1)
-        total = jnp.dot(low, high_ref[:, span], preferred_element_type=F32)
-        total = total + jnp.dot(high, low_ref[:, span], preferred_element_type=F32)
-        return total + jnp.dot(high, high_ref[:, span], preferred_element_type=F32)
+        outs = []
+        for at in range(0, high.shape[0], HALF):
+            some = slice(at, at + HALF)
+            total = jnp.dot(low[some], high_ref[:, span], preferred_element_type=F32)
+            total = total + jnp.dot(high[some], low_ref[:, span], preferred_element_type=F32)
+            outs.append(total + jnp.dot(high[some], high_ref[:, span], preferred_element_type=F32))
+        return jnp.concatenate(outs, axis=0)
 
     @pl.when(first_id >= near)
     def _():
@@ -221,7 +229,7 @@
             pl.BlockSpec(memory_space=pltpu.VMEM),
         ],
         out_specs=pl.BlockSpec((2, NB, width), lambda y: (0, y, 0)),
-        compiler_params=pltpu.CompilerParams(vmem_limit_bytes=57 * 2**20),
+        compiler_params=pltpu.CompilerParams(vmem_limit_bytes=50 * 2**20),
         cost_estimate=pl.CostEstimate(flops=5 * 10**9, bytes_accessed=16 * 2**20, transcendentals=0),
         name="update",
     )(place, pairs, gathered, high, low).reshape(rows, width)
@@ -261,7 +269,7 @@
     return jnp.stack([pick(received, my_z - my_row - k) for k in range(PANELS)])
 
 
-def scatter_lead(strip, my_x, my_core):
+def scatter_lead(strip, my_x, my_core, my_z):
     pieces = strip[:, 0:NB].reshape(N_X, N_CORE, PIECE, NB)
     keep = lax.dynamic_index_in_dim(pieces, my_core, 1, keepdims=False)
     give = lax.dynamic_index_in_dim(pieces, 1 - my_core, 1, keepdims=False)
@@ -279,7 +287,8 @@
         ]
         received.append(send(pick(both, my_x + step), pairs))
     received = jnp.stack(received)
-    return jnp.concatenate([pick(received, my_x), pick(received, my_x - 1)[0:1]], axis=0)
+    parts = jnp.concatenate([pick(received, my_x), pick(received, my_x - 1)[0:1]], axis=0)
+    return jnp.stack([pick(parts, my_z), pick(parts, my_z + 1)])
 
 
 def spread_lead(parts, my_z):
@@ -298,7 +307,7 @@
         received.append(send(hold, pairs))
     received = jnp.stack(received)
     spread = [pick(received, my_z - j) for j in range(PANELS)]
-    return jnp.stack([spread[j][k] for k, j in BLOCKS])
+    return jnp.stack(spread, axis=1).reshape(len(BLOCKS), PIECE, NB)
 
 
 def share_lead(mine, my_x, my_y):
@@ -357,7 +366,7 @@
     my_col = my_y * N_Z + my_z
     place = jnp.stack([my_row, my_col, jnp.int32(N_ROW), jnp.int32(N_COL)]).astype(jnp.int32)
     strip = kernel[0:NB]
-    parts = scatter_lead(strip, my_x, my_core)
+    parts = scatter_lead(strip, my_x, my_core, my_z)
     strip, parts = lax.optimization_barrier((strip, parts))
     mine = scatter_rows(strip, my_row, my_y, my_z)
     eighth = spread_lead(parts, my_z)

time: 170 us -> 155 us (0.912); the launches traced: 167 us -> 154 us
  Pallas kernels: 48 us -> 40.1 us
  waiting for transfers between devices: 73.8 us -> 67.1 us
  starting transfers between devices: 23.7 us -> 27.3 us
  local copies, waits for them, and re-layouts: 4.4 us -> 2.52 us
    pallas_call x1, Pallas kernels: 33.4 us -> 27 us  [factor_lead(): pl.pallas_call(factor_kernel, out_shape=[jax.ShapeDtypeStruct((LEAD, LEAD...]
    ppermute x21, waiting for transfers between devices: 64 us -> 59.8 us  [send(): return lax.ppermute(value, AXES, pairs)]
    ppermute x3, starting transfers between devices: 2.47 us -> 5.67 us  [share_lead(): lax.ppermute(mine, 'x', [(x, (x + step) % N_X) for x in range(N_X)])]
    ppermute x3, waiting for transfers between devices: 6.33 us -> 3.83 us  [share_lead(): lax.ppermute(mine, 'x', [(x, (x + step) % N_X) for x in range(N_X)])]
    unnamed x18 -> x7, local copies, waits for them, and re-layouts: 1.93 us -> 0.05 us
  transfers between devices with their start and end apart: 29 -> 29, of which waited for: 12 -> 11; matrix products, arithmetic and copies ran while one was open for 2% -> 2% of each run, Pallas kernels for 23% -> 20%
where the time goes in v1:
time: 155 us; the launch traced here: 154 us
  waiting for transfers between devices  67.1 us (43%)
  Pallas kernels  40.1 us (26%)
  starting transfers between devices  27.3 us (18%)
  between operations  14.3 us (9%)
  other arithmetic  2.92 us (2%)
  local copies, waits for them, and re-layouts  2.52 us (2%)
    ppermute x21, waiting for transfers between devices, send(): return lax.ppermute(value, AXES, pairs)  59.8 us
    pallas_call x1, Pallas kernels, factor_lead(): pl.pallas_call(factor_kernel, out_shape=[jax.ShapeDtypeStruct((LEAD, LEAD...  27 us
    ppermute x21, starting transfers between devices, send(): return lax.ppermute(value, AXES, pairs)  17.1 us
    pallas_call x1, Pallas kernels, update(): pl.pallas_call(update_kernel, grid=(rows // NB // 2,), out_shape=jax.Shap...  8.51 us
    ppermute x3, starting transfers between devices, share_lead(): lax.ppermute(mine, 'x', [(x, (x + step) % N_X) for x in range(N_X)])  5.67 us
    pallas_call x1, Pallas kernels, solve_lead(): pl.pallas_call(solve_kernel, out_shape=[jax.ShapeDtypeStruct((LEAD, width...  4.54 us
    ppermute x3, waiting for transfers between devices, share_lead(): lax.ppermute(mine, 'x', [(x, (x + step) % N_X) for x in range(N_X)])  3.83 us
  transfers between devices with their start and end apart: 29, of which 11 were waited for; matrix products, arithmetic and copies ran while one was open for 2% of the time, Pallas kernels for 20%

profile of v1, /device:TPU:21, one launch (start us, length us, event | category | flops | bytes accessed | tf_op | source)
XLA Modules:
  0.0 154.3 jit_solution(4717860389274893984)
XLA Ops:
  6.5 1.0 slice.14
  7.5 0.8 collective-permute-start
  8.3 1.0 collective-permute-done
  9.3 0.7 collective-permute-start.1
  10.0 0.7 collective-permute-start.2
  10.7 0.7 collective-permute-start.3
  11.4 1.1 slice.13
  12.6 0.0 collective-permute-done.1
  12.7 0.0 collective-permute-done.3
  12.8 0.2 copy.22
  13.0 0.1 dynamic-slice_bitcast_fusion.4
  13.1 0.7 collective-permute-start.4
  13.8 1.3 collective-permute-start.5
  15.1 1.3 collective-permute-start.6
  16.4 1.3 collective-permute-start.7
  17.7 0.7 collective-permute-start.8
  18.4 0.7 collective-permute-start.9
  19.1 10.2 %collective-permute-done.5 = f32[64,256]{1,0:T(8,128)S(1)} collective-permute-done((f32[64,256]{1,0:T(8,128)S(1)}, f32[64,256]{1,0:T(8,128)S(1)}, u32[]{:S(2)}, u32[]{:S(2)}) %collective-permute-start.5) | collective-permute-done | bytes 65568 | tf_op jit(solution)/shard_map/ppermute | solution.py:250
  29.2 0.7 collective-permute-start.10
  29.9 4.4 %collective-permute-done.6 = f32[64,256]{1,0:T(8,128)S(1)} collective-permute-done((f32[64,256]{1,0:T(8,128)S(1)}, f32[64,256]{1,0:T(8,128)S(1)}, u32[]{:S(2)}, u32[]{:S(2)}) %collective-permute-start.6) | collective-permute-done | bytes 65568 | tf_op jit(solution)/shard_map/ppermute | solution.py:250
  34.3 0.7 collective-permute-start.11
  35.0 2.5 %collective-permute-done.7 = f32[64,256]{1,0:T(8,128)S(1)} collective-permute-done((f32[64,256]{1,0:T(8,128)S(1)}, f32[64,256]{1,0:T(8,128)S(1)}, u32[]{:S(2)}, u32[]{:S(2)}) %collective-permute-start.7) | collective-permute-done | bytes 65568 | tf_op jit(solution)/shard_map/ppermute | solution.py:250
  37.5 0.0 collective-permute-done.8
  37.6 0.0 collective-permute-done.11
  37.6 0.7 pad_maximum_fusion.6
  38.3 0.0 all-gather.3.cloned.1.call-update
  38.3 0.7 collective-permute-start.12
  39.0 0.7 collective-permute-start.16
  39.7 0.7 collective-permute-start.17
  40.4 0.7 collective-permute-start.13
  41.1 0.7 collective-permute-start.14
  41.8 0.7 collective-permute-start.15
  42.6 0.7 collective-permute-start.18
  43.3 1.3 collective-permute-start.19
  44.6 0.7 collective-permute-start.20
  45.3 31.5 %collective-permute-done.19 = f32[6,32,256]{2,1,0:T(8,128)S(1)} collective-permute-done((f32[6,32,256]{2,1,0:T(8,128)S(1)}, f32[6,32,256]{2,1,0:T(8,128)S(1)}, u32[]{:S(2)}, u32[]{:S(2)}) %collective-permute-start.19) | collective-permute-done | bytes 196640 | tf_op jit(solution)/shard_map/ppermute | solution.py:250
  76.9 0.1 add_select_fusion
  76.9 2.5 %collective-permute-start.21 = (f32[6,32,256]{2,1,0:T(8,128)S(1)}, f32[6,32,256]{2,1,0:T(8,128)S(1)}, u32[]{:S(2)}, u32[]{:S(2)}) collective-permute-start(f32[6,32,256]{2,1,0:T(8,128)S(1)} %add_select_fusion), channel_id=1, source_target_pairs={{0,64},{64,128},{128,192},{192,0},{1,65},{65,129},{129,193},{193,1... | collective-permute-start | bytes 589832 | tf_op jit(solution)/shard_map/ppermute | solution.py:320
  79.4 1.2 collective-permute-start.22
  80.6 2.0 %collective-permute-start.23 = (f32[6,32,256]{2,1,0:T(8,128)S(1)}, f32[6,32,256]{2,1,0:T(8,128)S(1)}, u32[]{:S(2)}, u32[]{:S(2)}) collective-permute-start(f32[6,32,256]{2,1,0:T(8,128)S(1)} %add_select_fusion), channel_id=1, source_target_pairs={{0,192},{64,0},{128,64},{192,128},{1,193},{65,1},{129,65},{193,129... | collective-permute-start | bytes 589832 | tf_op jit(solution)/shard_map/ppermute | solution.py:320
  82.6 1.3 collective-permute-start.24
  83.9 3.2 %collective-permute-done.22 = f32[6,32,256]{2,1,0:T(8,128)S(1)} collective-permute-done((f32[6,32,256]{2,1,0:T(8,128)S(1)}, f32[6,32,256]{2,1,0:T(8,128)S(1)}, u32[]{:S(2)}, u32[]{:S(2)}) %collective-permute-start.22) | collective-permute-done | bytes 196640 | tf_op jit(solution)/shard_map/ppermute | solution.py:320
  87.1 0.6 collective-permute-done.23
  87.8 0.1 pad_maximum_fusion.2
  87.8 0.1 constant_dynamic-slice_fusion.3
  87.9 0.1 pad_maximum_fusion.3
  88.0 11.2 %collective-permute-done.24 = f32[256,512]{1,0:T(8,128)} collective-permute-done((f32[256,512]{1,0:T(8,128)S(1)}, f32[256,512]{1,0:T(8,128)}, u32[]{:S(2)}, u32[]{:S(2)}) %collective-permute-start.24) | collective-permute-done | bytes 524320 | tf_op jit(solution)/shard_map/ppermute | solution.py:250
  99.1 1.3 select_select_fusion.1
  100.4 1.3 collective-permute-start.27
  101.7 2.1 %collective-permute-start.26 = (f32[256,512]{1,0:T(8,128)S(1)}, f32[256,512]{1,0:T(8,128)S(1)}, u32[]{:S(2)}, u32[]{:S(2)}) collective-permute-start(f32[256,512]{1,0:T(8,128)S(1)} %get-tuple-element.31), channel_id=1, source_target_pairs={{0,32},{32,0},{1,33},{33,1},{2,34},{34,2},{3,35},{35,3},{4,36},{36... | collective-permute-start | bytes 1572872 | tf_op jit(solution)/shard_map/ppermute | solution.py:354
  103.9 0.3 collective-permute-start.25
  104.1 0.1 pad_add_fusion.place_ref
  104.2 0.9 collective-permute-done.27
  105.1 0.1 broadcast_select_fusion
  105.2 0.7 collective-permute-done.26
  105.9 0.1 broadcast_select_fusion.2
  106.0 0.1 pad_maximum_fusion.1.cols_ref
  106.1 0.9 collective-permute-done.25
  107.0 0.2 select_bitcast_fusion.1
  107.2 0.1 pad_maximum_fusion
  107.3 27.0 %factor_lead.1 = (f32[768,768]{1,0:T(8,128)S(1)}, f32[768,256]{1,0:T(8,128)S(1)}) custom-call(f32[8,6,32,256]{3,2,1,0:T(8,128)S(1)} %bitcast.94), custom_call_target="tpu_custom_call" | custom-call | flops 20000000000 | bytes 6291456 | tf_op jit(solution)/shard_map/factor_lead/pallas_call | solution.py:118
  134.3 4.5 %solve_lead.1 = (bf16[768,512]{1,0:T(8,128)(2,1)S(1)}, bf16[768,512]{1,0:T(8,128)(2,1)S(1)}) custom-call(s32[4]{0:T(128)S(1)} %pad_add_fusion.place_ref, f32[768,768]{1,0:T(8,128)S(1)} %get-tuple-element.25.work, f32[768,256]{1,0:T(8,128)S(1)} %get-tuple-element.26.inv, f32[768,512]{1,0:T(8,128)S(1)} %pad_maximum_fusion.1.cols_ref), custom_call_target="tpu_custom_call" | custom-call | flops 8000000000 | bytes 6291456 | tf_op jit(solution)/shard_map/solve_lead/pallas_call | solution.py:160
  138.9 0.0 all-gather.3.cloned.1.call-done
  138.9 8.5 %update.1 = f32[2,1024,512]{2,1,0:T(8,128)} custom-call(s32[4]{0:T(128)S(1)} %pad_add_fusion.place_ref, f32[2,1024,512]{2,1,0:T(8,128)} %bitcast.108, f32[4,8,3,64,256]{4,3,2,1,0:T(8,128)} %bitcast.115, bf16[768,512]{1,0:T(8,128)(2,1)S(1)} %get-tuple-element.29.high_ref, bf16[768,512]{1,0:T(8,128)(2,1)S(1)} %get-tuple-element.30.low_ref), custom_call_target="tpu_custom_call" | custom-call | flops 5000000000 | bytes 16777216 | tf_op jit(solution)/shard_map/update/pallas_call | solution.py:220
  (35 shorter events, 0.3 us)
Async XLA Ops:
  6.5 132.4 %all-gather.3.cloned.1.call-start = ((), (), s32[]{:S(2)}) async-start(), calls=%async_computation | async-start | bytes 6488064 | tf_op jit(solution)/shard_map/all_gather | solution.py:374
  7.5 1.7 %collective-permute-start = (f32[4,32,256]{2,1,0:T(8,128)S(1)}, f32[4,32,256]{2,1,0:T(8,128)S(1)}, u32[]{:S(2)}, u32[]{:S(2)}) collective-permute-start(f32[4,32,256]{2,1,0:T(8,128)S(1)} %dynamic-slice_bitcast_fusion), channel_id=1, source_target_pairs={{0,32},{32,0},{1,33},{33,1},{2,34},{34,2},{3,35},{35,3},{4,36},{36... | collective-permute-start | bytes 393224 | tf_op jit(solution)/shard_map/ppermute | solution.py:276
  9.3 3.3 %collective-permute-start.1 = (f32[2,32,256]{2,1,0:T(8,128)S(1)}, f32[2,32,256]{2,1,0:T(8,128)S(1)}, u32[]{:S(2)}, u32[]{:S(2)}) collective-permute-start(f32[2,32,256]{2,1,0:T(8,128)S(1)} %get-tuple-element.58), channel_id=1, source_target_pairs={{0,64},{1,65},{2,66},{32,96},{33,97},{34,98},{64,128},{65,129},{66... | collective-permute-start | bytes 196616 | tf_op jit(solution)/shard_map/ppermute | solution.py:250
  10.0 2.6 %collective-permute-start.2 = (f32[2,32,256]{2,1,0:T(8,128)S(1)}, f32[2,32,256]{2,1,0:T(8,128)S(1)}, u32[]{:S(2)}, u32[]{:S(2)}) collective-permute-start(f32[2,32,256]{2,1,0:T(8,128)S(1)} %get-tuple-element.59), channel_id=1, source_target_pairs={{0,128},{1,129},{2,130},{32,160},{33,161},{34,162},{64,192},{65,19... | collective-permute-start | bytes 196616 | tf_op jit(solution)/shard_map/ppermute | solution.py:250
  10.7 2.0 %collective-permute-start.3 = (f32[2,32,256]{2,1,0:T(8,128)S(1)}, f32[2,32,256]{2,1,0:T(8,128)S(1)}, u32[]{:S(2)}, u32[]{:S(2)}) collective-permute-start(f32[2,32,256]{2,1,0:T(8,128)S(1)} %get-tuple-element.60), channel_id=1, source_target_pairs={{0,192},{1,193},{2,194},{32,224},{33,225},{34,226},{64,0},{65,1},{... | collective-permute-start | bytes 196616 | tf_op jit(solution)/shard_map/ppermute | solution.py:250
  13.1 5.3 %collective-permute-start.4 = (f32[64,256]{1,0:T(8,128)S(1)}, f32[64,256]{1,0:T(8,128)S(1)}, u32[]{:S(2)}, u32[]{:S(2)}) collective-permute-start(f32[64,256]{1,0:T(8,128)S(1)} %get-tuple-element.51), channel_id=1, source_target_pairs={{0,0},{1,33},{2,66},{3,99},{4,132},{5,165},{6,198},{7,231},{8,8},{... | collective-permute-start | bytes 196616 | tf_op jit(solution)/shard_map/ppermute | solution.py:250
  13.8 15.4 %collective-permute-start.5 = (f32[64,256]{1,0:T(8,128)S(1)}, f32[64,256]{1,0:T(8,128)S(1)}, u32[]{:S(2)}, u32[]{:S(2)}) collective-permute-start(f32[64,256]{1,0:T(8,128)S(1)} %get-tuple-element.50), channel_id=1, source_target_pairs={{0,1},{1,34},{2,67},{3,100},{4,133},{5,166},{6,199},{7,224},{8,9},... | collective-permute-start | bytes 196616 | tf_op jit(solution)/shard_map/ppermute | solution.py:250
  15.1 19.2 %collective-permute-start.6 = (f32[64,256]{1,0:T(8,128)S(1)}, f32[64,256]{1,0:T(8,128)S(1)}, u32[]{:S(2)}, u32[]{:S(2)}) collective-permute-start(f32[64,256]{1,0:T(8,128)S(1)} %get-tuple-element.49), channel_id=1, source_target_pairs={{0,2},{1,35},{2,68},{3,101},{4,134},{5,167},{6,192},{7,225},{8,10}... | collective-permute-start | bytes 196616 | tf_op jit(solution)/shard_map/ppermute | solution.py:250
  16.4 21.1 %collective-permute-start.7 = (f32[64,256]{1,0:T(8,128)S(1)}, f32[64,256]{1,0:T(8,128)S(1)}, u32[]{:S(2)}, u32[]{:S(2)}) collective-permute-start(f32[64,256]{1,0:T(8,128)S(1)} %get-tuple-element.48), channel_id=1, source_target_pairs={{0,3},{1,36},{2,69},{3,102},{4,135},{5,160},{6,193},{7,226},{8,11}... | collective-permute-start | bytes 196616 | tf_op jit(solution)/shard_map/ppermute | solution.py:250
  17.7 19.8 %collective-permute-start.8 = (f32[64,256]{1,0:T(8,128)S(1)}, f32[64,256]{1,0:T(8,128)S(1)}, u32[]{:S(2)}, u32[]{:S(2)}) collective-permute-start(f32[64,256]{1,0:T(8,128)S(1)} %get-tuple-element.47), channel_id=1, source_target_pairs={{0,4},{1,37},{2,70},{3,103},{4,128},{5,161},{6,194},{7,227},{8,12}... | collective-permute-start | bytes 196616 | tf_op jit(solution)/shard_map/ppermute | solution.py:250
  18.4 19.1 %collective-permute-start.9 = (f32[64,256]{1,0:T(8,128)S(1)}, f32[64,256]{1,0:T(8,128)S(1)}, u32[]{:S(2)}, u32[]{:S(2)}) collective-permute-start(f32[64,256]{1,0:T(8,128)S(1)} %get-tuple-element.46), channel_id=1, source_target_pairs={{0,5},{1,38},{2,71},{3,96},{4,129},{5,162},{6,195},{7,228},{8,13},... | collective-permute-start | bytes 196616 | tf_op jit(solution)/shard_map/ppermute | solution.py:250
  29.2 8.3 %collective-permute-start.10 = (f32[64,256]{1,0:T(8,128)S(1)}, f32[64,256]{1,0:T(8,128)S(1)}, u32[]{:S(2)}, u32[]{:S(2)}) collective-permute-start(f32[64,256]{1,0:T(8,128)S(1)} %get-tuple-element.45), channel_id=1, source_target_pairs={{0,6},{1,39},{2,64},{3,97},{4,130},{5,163},{6,196},{7,229},{8,14},... | collective-permute-start | bytes 196616 | tf_op jit(solution)/shard_map/ppermute | solution.py:250
  34.3 3.2 %collective-permute-start.11 = (f32[64,256]{1,0:T(8,128)S(1)}, f32[64,256]{1,0:T(8,128)S(1)}, u32[]{:S(2)}, u32[]{:S(2)}) collective-permute-start(f32[64,256]{1,0:T(8,128)S(1)} %get-tuple-element.44), channel_id=1, source_target_pairs={{0,7},{1,32},{2,65},{3,98},{4,131},{5,164},{6,197},{7,230},{8,15},... | collective-permute-start | bytes 196616 | tf_op jit(solution)/shard_map/ppermute | solution.py:250
  38.3 2.1 %collective-permute-start.12 = (f32[2,32,256]{2,1,0:T(8,128)S(1)}, f32[2,32,256]{2,1,0:T(8,128)S(1)}, u32[]{:S(2)}, u32[]{:S(2)}) collective-permute-start(f32[2,32,256]{2,1,0:T(8,128)S(1)} %pad_maximum_fusion.8), channel_id=1, source_target_pairs={{0,4},{1,5},{2,6},{32,36},{33,37},{34,38},{64,68},{65,69},{66,70},... | collective-permute-start | bytes 196616 | tf_op jit(solution)/shard_map/ppermute | solution.py:250
  39.0 3.6 %collective-permute-start.16 = (f32[256,512]{1,0:T(8,128)S(1)}, f32[256,512]{1,0:T(8,128)S(1)}, u32[]{:S(2)}, u32[]{:S(2)}) collective-permute-start(f32[256,512]{1,0:T(8,128)S(1)} %slice.13), channel_id=1, source_target_pairs={{0,64},{1,65},{2,66},{3,67},{4,68},{5,69},{6,70},{7,71},{8,72},{9,... | collective-permute-start | bytes 1572872 | tf_op jit(solution)/shard_map/ppermute | solution.py:250
  39.7 2.9 %collective-permute-start.17 = (f32[256,512]{1,0:T(8,128)S(1)}, f32[256,512]{1,0:T(8,128)S(1)}, u32[]{:S(2)}, u32[]{:S(2)}) collective-permute-start(f32[256,512]{1,0:T(8,128)S(1)} %slice.13), channel_id=1, source_target_pairs={{0,192},{1,193},{2,194},{3,195},{4,196},{5,197},{6,198},{7,199},{8... | collective-permute-start | bytes 1572872 | tf_op jit(solution)/shard_map/ppermute | solution.py:250
  40.4 2.1 %collective-permute-start.13 = (f32[2,32,256]{2,1,0:T(8,128)S(1)}, f32[2,32,256]{2,1,0:T(8,128)S(1)}, u32[]{:S(2)}, u32[]{:S(2)}) collective-permute-start(f32[2,32,256]{2,1,0:T(8,128)S(1)} %broadcast_select_fusion.3), channel_id=1, source_target_pairs={{0,1},{4,5},{1,2},{5,6},{2,3},{6,7},{32,33},{36,37},{33,34},{37,38... | collective-permute-start | bytes 196616 | tf_op jit(solution)/shard_map/ppermute | solution.py:250
  41.1 1.4 collective-permute-start.14
  41.8 0.8 collective-permute-start.15
  42.6 2.7 %collective-permute-start.18 = (f32[6,32,256]{2,1,0:T(8,128)S(1)}, f32[6,32,256]{2,1,0:T(8,128)S(1)}, u32[]{:S(2)}, u32[]{:S(2)}) collective-permute-start(f32[6,32,256]{2,1,0:T(8,128)S(1)} %bitcast.100), channel_id=1, source_target_pairs={{0,8},{1,9},{2,10},{3,11},{4,12},{5,13},{6,14},{7,15},{32,40},{33,... | collective-permute-start | bytes 589832 | tf_op jit(solution)/shard_map/ppermute | solution.py:250
  43.3 33.5 %collective-permute-start.19 = (f32[6,32,256]{2,1,0:T(8,128)S(1)}, f32[6,32,256]{2,1,0:T(8,128)S(1)}, u32[]{:S(2)}, u32[]{:S(2)}) collective-permute-start(f32[6,32,256]{2,1,0:T(8,128)S(1)} %bitcast.101), channel_id=1, source_target_pairs={{0,16},{1,17},{2,18},{3,19},{4,20},{5,21},{6,22},{7,23},{32,48},{3... | collective-permute-start | bytes 589832 | tf_op jit(solution)/shard_map/ppermute | solution.py:250
  44.6 32.2 %collective-permute-start.20 = (f32[6,32,256]{2,1,0:T(8,128)S(1)}, f32[6,32,256]{2,1,0:T(8,128)S(1)}, u32[]{:S(2)}, u32[]{:S(2)}) collective-permute-start(f32[6,32,256]{2,1,0:T(8,128)S(1)} %bitcast.102), channel_id=1, source_target_pairs={{0,24},{1,25},{2,26},{3,27},{4,28},{5,29},{6,30},{7,31},{32,56},{3... | collective-permute-start | bytes 589832 | tf_op jit(solution)/shard_map/ppermute | solution.py:250
  76.9 7.0 %collective-permute-start.21 = (f32[6,32,256]{2,1,0:T(8,128)S(1)}, f32[6,32,256]{2,1,0:T(8,128)S(1)}, u32[]{:S(2)}, u32[]{:S(2)}) collective-permute-start(f32[6,32,256]{2,1,0:T(8,128)S(1)} %add_select_fusion), channel_id=1, source_target_pairs={{0,64},{64,128},{128,192},{192,0},{1,65},{65,129},{129,193},{193,1... | collective-permute-start | bytes 589832 | tf_op jit(solution)/shard_map/ppermute | solution.py:320
  79.4 7.7 %collective-permute-start.22 = (f32[6,32,256]{2,1,0:T(8,128)S(1)}, f32[6,32,256]{2,1,0:T(8,128)S(1)}, u32[]{:S(2)}, u32[]{:S(2)}) collective-permute-start(f32[6,32,256]{2,1,0:T(8,128)S(1)} %add_select_fusion), channel_id=1, source_target_pairs={{0,128},{64,192},{128,0},{192,64},{1,129},{65,193},{129,1},{193,65... | collective-permute-start | bytes 589832 | tf_op jit(solution)/shard_map/ppermute | solution.py:320
  80.6 7.1 %collective-permute-start.23 = (f32[6,32,256]{2,1,0:T(8,128)S(1)}, f32[6,32,256]{2,1,0:T(8,128)S(1)}, u32[]{:S(2)}, u32[]{:S(2)}) collective-permute-start(f32[6,32,256]{2,1,0:T(8,128)S(1)} %add_select_fusion), channel_id=1, source_target_pairs={{0,192},{64,0},{128,64},{192,128},{1,193},{65,1},{129,65},{193,129... | collective-permute-start | bytes 589832 | tf_op jit(solution)/shard_map/ppermute | solution.py:320
  82.6 16.6 %collective-permute-start.24 = (f32[256,512]{1,0:T(8,128)S(1)}, f32[256,512]{1,0:T(8,128)}, u32[]{:S(2)}, u32[]{:S(2)}) collective-permute-start(f32[256,512]{1,0:T(8,128)S(1)} %collective-permute-done.16), channel_id=1, source_target_pairs={{64,128},{65,129},{66,130},{67,131},{68,132},{69,133},{70,134},{71... | collective-permute-start | bytes 1572872 | tf_op jit(solution)/shard_map/ppermute | solution.py:250
  100.4 4.7 %collective-permute-start.27 = (f32[256,512]{1,0:T(8,128)S(1)}, f32[256,512]{1,0:T(8,128)S(1)}, u32[]{:S(2)}, u32[]{:S(2)}) collective-permute-start(f32[256,512]{1,0:T(8,128)S(1)} %get-tuple-element.32), channel_id=1, source_target_pairs={{0,32},{1,33},{2,34},{3,35},{4,36},{5,37},{6,38},{7,39},{8,40},{9,... | collective-permute-start | bytes 1572872 | tf_op jit(solution)/shard_map/ppermute | solution.py:355
  101.7 4.1 %collective-permute-start.26 = (f32[256,512]{1,0:T(8,128)S(1)}, f32[256,512]{1,0:T(8,128)S(1)}, u32[]{:S(2)}, u32[]{:S(2)}) collective-permute-start(f32[256,512]{1,0:T(8,128)S(1)} %get-tuple-element.31), channel_id=1, source_target_pairs={{0,32},{32,0},{1,33},{33,1},{2,34},{34,2},{3,35},{35,3},{4,36},{36... | collective-permute-start | bytes 1572872 | tf_op jit(solution)/shard_map/ppermute | solution.py:354
  103.9 3.1 %collective-permute-start.25 = (f32[4,6,32,256]{3,2,1,0:T(8,128)S(1)}, f32[4,6,32,256]{3,2,1,0:T(8,128)S(1)}, u32[]{:S(2)}, u32[]{:S(2)}) collective-permute-start(f32[4,6,32,256]{3,2,1,0:T(8,128)S(1)} %pad_maximum_fusion.3), channel_id=1, source_target_pairs={{0,32},{32,0},{1,33},{33,1},{2,34},{34,2},{3,35},{35,3},{4,36},{36... | collective-permute-start | bytes 2359304 | tf_op jit(solution)/shard_map/ppermute | solution.py:327
Sparse Core Ops, SparseCore 0:
  38.4 89.4 all-gather.2

commit v2 on v1

--- a/solution.py
+++ b/solution.py
@@ -110,7 +110,12 @@
                 below = slice((done + 1) * HALF, LEAD)
                 factor = dot_split(work[below, here], inverse, 1, 1)
                 work[below, here] = factor
-                work[below, below] = work[below, below] - dot_split(factor, factor, 1, 1)
+                for first in range(below.start, LEAD, NB):
+                    rows = slice(first, LEAD)
+                    lanes = slice(first, min(first + NB, LEAD))
+                    left = factor[first - below.start :]
+                    right = factor[first - below.start : lanes.stop - below.start]
+                    work[rows, lanes] = work[rows, lanes] - dot_split(left, right, 1, 1)
 
 
 def factor_lead(lead):

time: 155 us -> 155 us (level)
  no operation moved by 1% of the time
where the time goes in v2:
time: 155 us; the launch traced here: 154 us
  waiting for transfers between devices  67.1 us (43%)
  Pallas kernels  39.7 us (26%)
  starting transfers between devices  27.3 us (18%)
  between operations  14.3 us (9%)
  other arithmetic  2.92 us (2%)
  local copies, waits for them, and re-layouts  2.52 us (2%)
    ppermute x21, waiting for transfers between devices, send(): return lax.ppermute(value, AXES, pairs)  59.8 us
    pallas_call x1, Pallas kernels, factor_lead(): pl.pallas_call(factor_kernel, out_shape=[jax.ShapeDtypeStruct((LEAD, LEAD...  26.7 us
    ppermute x21, starting transfers between devices, send(): return lax.ppermute(value, AXES, pairs)  17.1 us
    pallas_call x1, Pallas kernels, update(): pl.pallas_call(update_kernel, grid=(rows // NB // 2,), out_shape=jax.Shap...  8.51 us
    ppermute x3, starting transfers between devices, share_lead(): lax.ppermute(mine, 'x', [(x, (x + step) % N_X) for x in range(N_X)])  5.67 us
    pallas_call x1, Pallas kernels, solve_lead(): pl.pallas_call(solve_kernel, out_shape=[jax.ShapeDtypeStruct((LEAD, width...  4.54 us
    ppermute x3, waiting for transfers between devices, share_lead(): lax.ppermute(mine, 'x', [(x, (x + step) % N_X) for x in range(N_X)])  3.83 us
  transfers between devices with their start and end apart: 29, of which 11 were waited for; matrix products, arithmetic and copies ran while one was open for 2% of the time, Pallas kernels for 20%

profile of v2, /device:TPU:21, one launch (start us, length us, event | category | flops | bytes accessed | tf_op | source)
XLA Modules:
  0.0 153.9 jit_solution(17496360708284163514)
XLA Ops:
  6.5 1.0 slice.14
  7.5 0.8 collective-permute-start
  8.3 1.0 collective-permute-done
  9.3 0.7 collective-permute-start.1
  10.0 0.7 collective-permute-start.2
  10.7 0.7 collective-permute-start.3
  11.4 1.1 slice.13
  12.6 0.0 collective-permute-done.1
  12.7 0.0 collective-permute-done.3
  12.8 0.2 copy.22
  13.0 0.1 dynamic-slice_bitcast_fusion.4
  13.1 0.7 collective-permute-start.4
  13.8 1.3 collective-permute-start.5
  15.1 1.3 collective-permute-start.6
  16.4 1.3 collective-permute-start.7
  17.7 0.7 collective-permute-start.8
  18.4 0.7 collective-permute-start.9
  19.1 10.2 %collective-permute-done.5 = f32[64,256]{1,0:T(8,128)S(1)} collective-permute-done((f32[64,256]{1,0:T(8,128)S(1)}, f32[64,256]{1,0:T(8,128)S(1)}, u32[]{:S(2)}, u32[]{:S(2)}) %collective-permute-start.5) | collective-permute-done | bytes 65568 | tf_op jit(solution)/shard_map/ppermute | solution.py:255
  29.2 0.7 collective-permute-start.10
  29.9 4.4 %collective-permute-done.6 = f32[64,256]{1,0:T(8,128)S(1)} collective-permute-done((f32[64,256]{1,0:T(8,128)S(1)}, f32[64,256]{1,0:T(8,128)S(1)}, u32[]{:S(2)}, u32[]{:S(2)}) %collective-permute-start.6) | collective-permute-done | bytes 65568 | tf_op jit(solution)/shard_map/ppermute | solution.py:255
  34.3 0.7 collective-permute-start.11
  35.0 2.5 %collective-permute-done.7 = f32[64,256]{1,0:T(8,128)S(1)} collective-permute-done((f32[64,256]{1,0:T(8,128)S(1)}, f32[64,256]{1,0:T(8,128)S(1)}, u32[]{:S(2)}, u32[]{:S(2)}) %collective-permute-start.7) | collective-permute-done | bytes 65568 | tf_op jit(solution)/shard_map/ppermute | solution.py:255
  37.5 0.0 collective-permute-done.8
  37.6 0.0 collective-permute-done.11
  37.6 0.7 pad_maximum_fusion.6
  38.3 0.0 all-gather.3.cloned.1.call-update
  38.3 0.7 collective-permute-start.12
  39.0 0.7 collective-permute-start.16
  39.7 0.7 collective-permute-start.17
  40.4 0.7 collective-permute-start.13
  41.1 0.7 collective-permute-start.14
  41.8 0.7 collective-permute-start.15
  42.6 0.7 collective-permute-start.18
  43.3 1.3 collective-permute-start.19
  44.6 0.7 collective-permute-start.20
  45.3 31.5 %collective-permute-done.19 = f32[6,32,256]{2,1,0:T(8,128)S(1)} collective-permute-done((f32[6,32,256]{2,1,0:T(8,128)S(1)}, f32[6,32,256]{2,1,0:T(8,128)S(1)}, u32[]{:S(2)}, u32[]{:S(2)}) %collective-permute-start.19) | collective-permute-done | bytes 196640 | tf_op jit(solution)/shard_map/ppermute | solution.py:255
  76.9 0.1 add_select_fusion
  76.9 2.5 %collective-permute-start.21 = (f32[6,32,256]{2,1,0:T(8,128)S(1)}, f32[6,32,256]{2,1,0:T(8,128)S(1)}, u32[]{:S(2)}, u32[]{:S(2)}) collective-permute-start(f32[6,32,256]{2,1,0:T(8,128)S(1)} %add_select_fusion), channel_id=1, source_target_pairs={{0,64},{64,128},{128,192},{192,0},{1,65},{65,129},{129,193},{193,1... | collective-permute-start | bytes 589832 | tf_op jit(solution)/shard_map/ppermute | solution.py:325
  79.4 1.2 collective-permute-start.22
  80.6 2.0 %collective-permute-start.23 = (f32[6,32,256]{2,1,0:T(8,128)S(1)}, f32[6,32,256]{2,1,0:T(8,128)S(1)}, u32[]{:S(2)}, u32[]{:S(2)}) collective-permute-start(f32[6,32,256]{2,1,0:T(8,128)S(1)} %add_select_fusion), channel_id=1, source_target_pairs={{0,192},{64,0},{128,64},{192,128},{1,193},{65,1},{129,65},{193,129... | collective-permute-start | bytes 589832 | tf_op jit(solution)/shard_map/ppermute | solution.py:325
  82.6 1.3 collective-permute-start.24
  83.9 3.2 %collective-permute-done.22 = f32[6,32,256]{2,1,0:T(8,128)S(1)} collective-permute-done((f32[6,32,256]{2,1,0:T(8,128)S(1)}, f32[6,32,256]{2,1,0:T(8,128)S(1)}, u32[]{:S(2)}, u32[]{:S(2)}) %collective-permute-start.22) | collective-permute-done | bytes 196640 | tf_op jit(solution)/shard_map/ppermute | solution.py:325
  87.1 0.6 collective-permute-done.23
  87.8 0.1 pad_maximum_fusion.2
  87.8 0.1 constant_dynamic-slice_fusion.3
  87.9 0.1 pad_maximum_fusion.3
  88.0 11.2 %collective-permute-done.24 = f32[256,512]{1,0:T(8,128)} collective-permute-done((f32[256,512]{1,0:T(8,128)S(1)}, f32[256,512]{1,0:T(8,128)}, u32[]{:S(2)}, u32[]{:S(2)}) %collective-permute-start.24) | collective-permute-done | bytes 524320 | tf_op jit(solution)/shard_map/ppermute | solution.py:255
  99.1 1.3 select_select_fusion.1
  100.4 1.3 collective-permute-start.27
  101.7 2.1 %collective-permute-start.26 = (f32[256,512]{1,0:T(8,128)S(1)}, f32[256,512]{1,0:T(8,128)S(1)}, u32[]{:S(2)}, u32[]{:S(2)}) collective-permute-start(f32[256,512]{1,0:T(8,128)S(1)} %get-tuple-element.31), channel_id=1, source_target_pairs={{0,32},{32,0},{1,33},{33,1},{2,34},{34,2},{3,35},{35,3},{4,36},{36... | collective-permute-start | bytes 1572872 | tf_op jit(solution)/shard_map/ppermute | solution.py:359
  103.9 0.3 collective-permute-start.25
  104.1 0.1 pad_add_fusion.place_ref
  104.2 0.9 collective-permute-done.27
  105.1 0.1 broadcast_select_fusion
  105.2 0.7 collective-permute-done.26
  105.9 0.1 broadcast_select_fusion.2
  106.0 0.1 pad_maximum_fusion.1.cols_ref
  106.1 0.9 collective-permute-done.25
  107.0 0.2 select_bitcast_fusion.1
  107.2 0.1 pad_maximum_fusion
  107.3 26.7 %factor_lead.1 = (f32[768,768]{1,0:T(8,128)S(1)}, f32[768,256]{1,0:T(8,128)S(1)}) custom-call(f32[8,6,32,256]{3,2,1,0:T(8,128)S(1)} %bitcast.94), custom_call_target="tpu_custom_call" | custom-call | flops 20000000000 | bytes 6291456 | tf_op jit(solution)/shard_map/factor_lead/pallas_call | solution.py:123
  133.9 4.5 %solve_lead.1 = (bf16[768,512]{1,0:T(8,128)(2,1)S(1)}, bf16[768,512]{1,0:T(8,128)(2,1)S(1)}) custom-call(s32[4]{0:T(128)S(1)} %pad_add_fusion.place_ref, f32[768,768]{1,0:T(8,128)S(1)} %get-tuple-element.25.work, f32[768,256]{1,0:T(8,128)S(1)} %get-tuple-element.26.inv, f32[768,512]{1,0:T(8,128)S(1)} %pad_maximum_fusion.1.cols_ref), custom_call_target="tpu_custom_call" | custom-call | flops 8000000000 | bytes 6291456 | tf_op jit(solution)/shard_map/solve_lead/pallas_call | solution.py:165
  138.5 0.0 all-gather.3.cloned.1.call-done
  138.5 8.5 %update.1 = f32[2,1024,512]{2,1,0:T(8,128)} custom-call(s32[4]{0:T(128)S(1)} %pad_add_fusion.place_ref, f32[2,1024,512]{2,1,0:T(8,128)} %bitcast.108, f32[4,8,3,64,256]{4,3,2,1,0:T(8,128)} %bitcast.115, bf16[768,512]{1,0:T(8,128)(2,1)S(1)} %get-tuple-element.29.high_ref, bf16[768,512]{1,0:T(8,128)(2,1)S(1)} %get-tuple-element.30.low_ref), custom_call_target="tpu_custom_call" | custom-call | flops 5000000000 | bytes 16777216 | tf_op jit(solution)/shard_map/update/pallas_call | solution.py:225
  (35 shorter events, 0.3 us)
Async XLA Ops:
  6.5 132.0 %all-gather.3.cloned.1.call-start = ((), (), s32[]{:S(2)}) async-start(), calls=%async_computation | async-start | bytes 6488064 | tf_op jit(solution)/shard_map/all_gather | solution.py:379
  7.5 1.7 %collective-permute-start = (f32[4,32,256]{2,1,0:T(8,128)S(1)}, f32[4,32,256]{2,1,0:T(8,128)S(1)}, u32[]{:S(2)}, u32[]{:S(2)}) collective-permute-start(f32[4,32,256]{2,1,0:T(8,128)S(1)} %dynamic-slice_bitcast_fusion), channel_id=1, source_target_pairs={{0,32},{32,0},{1,33},{33,1},{2,34},{34,2},{3,35},{35,3},{4,36},{36... | collective-permute-start | bytes 393224 | tf_op jit(solution)/shard_map/ppermute | solution.py:281
  9.3 3.3 %collective-permute-start.1 = (f32[2,32,256]{2,1,0:T(8,128)S(1)}, f32[2,32,256]{2,1,0:T(8,128)S(1)}, u32[]{:S(2)}, u32[]{:S(2)}) collective-permute-start(f32[2,32,256]{2,1,0:T(8,128)S(1)} %get-tuple-element.58), channel_id=1, source_target_pairs={{0,64},{1,65},{2,66},{32,96},{33,97},{34,98},{64,128},{65,129},{66... | collective-permute-start | bytes 196616 | tf_op jit(solution)/shard_map/ppermute | solution.py:255
  10.0 2.6 %collective-permute-start.2 = (f32[2,32,256]{2,1,0:T(8,128)S(1)}, f32[2,32,256]{2,1,0:T(8,128)S(1)}, u32[]{:S(2)}, u32[]{:S(2)}) collective-permute-start(f32[2,32,256]{2,1,0:T(8,128)S(1)} %get-tuple-element.59), channel_id=1, source_target_pairs={{0,128},{1,129},{2,130},{32,160},{33,161},{34,162},{64,192},{65,19... | collective-permute-start | bytes 196616 | tf_op jit(solution)/shard_map/ppermute | solution.py:255
  10.7 2.0 %collective-permute-start.3 = (f32[2,32,256]{2,1,0:T(8,128)S(1)}, f32[2,32,256]{2,1,0:T(8,128)S(1)}, u32[]{:S(2)}, u32[]{:S(2)}) collective-permute-start(f32[2,32,256]{2,1,0:T(8,128)S(1)} %get-tuple-element.60), channel_id=1, source_target_pairs={{0,192},{1,193},{2,194},{32,224},{33,225},{34,226},{64,0},{65,1},{... | collective-permute-start | bytes 196616 | tf_op jit(solution)/shard_map/ppermute | solution.py:255
  13.1 5.3 %collective-permute-start.4 = (f32[64,256]{1,0:T(8,128)S(1)}, f32[64,256]{1,0:T(8,128)S(1)}, u32[]{:S(2)}, u32[]{:S(2)}) collective-permute-start(f32[64,256]{1,0:T(8,128)S(1)} %get-tuple-element.51), channel_id=1, source_target_pairs={{0,0},{1,33},{2,66},{3,99},{4,132},{5,165},{6,198},{7,231},{8,8},{... | collective-permute-start | bytes 196616 | tf_op jit(solution)/shard_map/ppermute | solution.py:255
  13.8 15.4 %collective-permute-start.5 = (f32[64,256]{1,0:T(8,128)S(1)}, f32[64,256]{1,0:T(8,128)S(1)}, u32[]{:S(2)}, u32[]{:S(2)}) collective-permute-start(f32[64,256]{1,0:T(8,128)S(1)} %get-tuple-element.50), channel_id=1, source_target_pairs={{0,1},{1,34},{2,67},{3,100},{4,133},{5,166},{6,199},{7,224},{8,9},... | collective-permute-start | bytes 196616 | tf_op jit(solution)/shard_map/ppermute | solution.py:255
  15.1 19.2 %collective-permute-start.6 = (f32[64,256]{1,0:T(8,128)S(1)}, f32[64,256]{1,0:T(8,128)S(1)}, u32[]{:S(2)}, u32[]{:S(2)}) collective-permute-start(f32[64,256]{1,0:T(8,128)S(1)} %get-tuple-element.49), channel_id=1, source_target_pairs={{0,2},{1,35},{2,68},{3,101},{4,134},{5,167},{6,192},{7,225},{8,10}... | collective-permute-start | bytes 196616 | tf_op jit(solution)/shard_map/ppermute | solution.py:255
  16.4 21.1 %collective-permute-start.7 = (f32[64,256]{1,0:T(8,128)S(1)}, f32[64,256]{1,0:T(8,128)S(1)}, u32[]{:S(2)}, u32[]{:S(2)}) collective-permute-start(f32[64,256]{1,0:T(8,128)S(1)} %get-tuple-element.48), channel_id=1, source_target_pairs={{0,3},{1,36},{2,69},{3,102},{4,135},{5,160},{6,193},{7,226},{8,11}... | collective-permute-start | bytes 196616 | tf_op jit(solution)/shard_map/ppermute | solution.py:255
  17.7 19.8 %collective-permute-start.8 = (f32[64,256]{1,0:T(8,128)S(1)}, f32[64,256]{1,0:T(8,128)S(1)}, u32[]{:S(2)}, u32[]{:S(2)}) collective-permute-start(f32[64,256]{1,0:T(8,128)S(1)} %get-tuple-element.47), channel_id=1, source_target_pairs={{0,4},{1,37},{2,70},{3,103},{4,128},{5,161},{6,194},{7,227},{8,12}... | collective-permute-start | bytes 196616 | tf_op jit(solution)/shard_map/ppermute | solution.py:255
  18.4 19.1 %collective-permute-start.9 = (f32[64,256]{1,0:T(8,128)S(1)}, f32[64,256]{1,0:T(8,128)S(1)}, u32[]{:S(2)}, u32[]{:S(2)}) collective-permute-start(f32[64,256]{1,0:T(8,128)S(1)} %get-tuple-element.46), channel_id=1, source_target_pairs={{0,5},{1,38},{2,71},{3,96},{4,129},{5,162},{6,195},{7,228},{8,13},... | collective-permute-start | bytes 196616 | tf_op jit(solution)/shard_map/ppermute | solution.py:255
  29.2 8.3 %collective-permute-start.10 = (f32[64,256]{1,0:T(8,128)S(1)}, f32[64,256]{1,0:T(8,128)S(1)}, u32[]{:S(2)}, u32[]{:S(2)}) collective-permute-start(f32[64,256]{1,0:T(8,128)S(1)} %get-tuple-element.45), channel_id=1, source_target_pairs={{0,6},{1,39},{2,64},{3,97},{4,130},{5,163},{6,196},{7,229},{8,14},... | collective-permute-start | bytes 196616 | tf_op jit(solution)/shard_map/ppermute | solution.py:255
  34.3 3.2 %collective-permute-start.11 = (f32[64,256]{1,0:T(8,128)S(1)}, f32[64,256]{1,0:T(8,128)S(1)}, u32[]{:S(2)}, u32[]{:S(2)}) collective-permute-start(f32[64,256]{1,0:T(8,128)S(1)} %get-tuple-element.44), channel_id=1, source_target_pairs={{0,7},{1,32},{2,65},{3,98},{4,131},{5,164},{6,197},{7,230},{8,15},... | collective-permute-start | bytes 196616 | tf_op jit(solution)/shard_map/ppermute | solution.py:255
  38.3 2.1 %collective-permute-start.12 = (f32[2,32,256]{2,1,0:T(8,128)S(1)}, f32[2,32,256]{2,1,0:T(8,128)S(1)}, u32[]{:S(2)}, u32[]{:S(2)}) collective-permute-start(f32[2,32,256]{2,1,0:T(8,128)S(1)} %pad_maximum_fusion.8), channel_id=1, source_target_pairs={{0,4},{1,5},{2,6},{32,36},{33,37},{34,38},{64,68},{65,69},{66,70},... | collective-permute-start | bytes 196616 | tf_op jit(solution)/shard_map/ppermute | solution.py:255
  39.0 3.6 %collective-permute-start.16 = (f32[256,512]{1,0:T(8,128)S(1)}, f32[256,512]{1,0:T(8,128)S(1)}, u32[]{:S(2)}, u32[]{:S(2)}) collective-permute-start(f32[256,512]{1,0:T(8,128)S(1)} %slice.13), channel_id=1, source_target_pairs={{0,64},{1,65},{2,66},{3,67},{4,68},{5,69},{6,70},{7,71},{8,72},{9,... | collective-permute-start | bytes 1572872 | tf_op jit(solution)/shard_map/ppermute | solution.py:255
  39.7 2.9 %collective-permute-start.17 = (f32[256,512]{1,0:T(8,128)S(1)}, f32[256,512]{1,0:T(8,128)S(1)}, u32[]{:S(2)}, u32[]{:S(2)}) collective-permute-start(f32[256,512]{1,0:T(8,128)S(1)} %slice.13), channel_id=1, source_target_pairs={{0,192},{1,193},{2,194},{3,195},{4,196},{5,197},{6,198},{7,199},{8... | collective-permute-start | bytes 1572872 | tf_op jit(solution)/shard_map/ppermute | solution.py:255
  40.4 2.1 %collective-permute-start.13 = (f32[2,32,256]{2,1,0:T(8,128)S(1)}, f32[2,32,256]{2,1,0:T(8,128)S(1)}, u32[]{:S(2)}, u32[]{:S(2)}) collective-permute-start(f32[2,32,256]{2,1,0:T(8,128)S(1)} %broadcast_select_fusion.3), channel_id=1, source_target_pairs={{0,1},{4,5},{1,2},{5,6},{2,3},{6,7},{32,33},{36,37},{33,34},{37,38... | collective-permute-start | bytes 196616 | tf_op jit(solution)/shard_map/ppermute | solution.py:255
  41.1 1.4 collective-permute-start.14
  41.8 0.8 collective-permute-start.15
  42.6 2.7 %collective-permute-start.18 = (f32[6,32,256]{2,1,0:T(8,128)S(1)}, f32[6,32,256]{2,1,0:T(8,128)S(1)}, u32[]{:S(2)}, u32[]{:S(2)}) collective-permute-start(f32[6,32,256]{2,1,0:T(8,128)S(1)} %bitcast.100), channel_id=1, source_target_pairs={{0,8},{1,9},{2,10},{3,11},{4,12},{5,13},{6,14},{7,15},{32,40},{33,... | collective-permute-start | bytes 589832 | tf_op jit(solution)/shard_map/ppermute | solution.py:255
  43.3 33.5 %collective-permute-start.19 = (f32[6,32,256]{2,1,0:T(8,128)S(1)}, f32[6,32,256]{2,1,0:T(8,128)S(1)}, u32[]{:S(2)}, u32[]{:S(2)}) collective-permute-start(f32[6,32,256]{2,1,0:T(8,128)S(1)} %bitcast.101), channel_id=1, source_target_pairs={{0,16},{1,17},{2,18},{3,19},{4,20},{5,21},{6,22},{7,23},{32,48},{3... | collective-permute-start | bytes 589832 | tf_op jit(solution)/shard_map/ppermute | solution.py:255
  44.6 32.2 %collective-permute-start.20 = (f32[6,32,256]{2,1,0:T(8,128)S(1)}, f32[6,32,256]{2,1,0:T(8,128)S(1)}, u32[]{:S(2)}, u32[]{:S(2)}) collective-permute-start(f32[6,32,256]{2,1,0:T(8,128)S(1)} %bitcast.102), channel_id=1, source_target_pairs={{0,24},{1,25},{2,26},{3,27},{4,28},{5,29},{6,30},{7,31},{32,56},{3... | collective-permute-start | bytes 589832 | tf_op jit(solution)/shard_map/ppermute | solution.py:255
  76.9 7.0 %collective-permute-start.21 = (f32[6,32,256]{2,1,0:T(8,128)S(1)}, f32[6,32,256]{2,1,0:T(8,128)S(1)}, u32[]{:S(2)}, u32[]{:S(2)}) collective-permute-start(f32[6,32,256]{2,1,0:T(8,128)S(1)} %add_select_fusion), channel_id=1, source_target_pairs={{0,64},{64,128},{128,192},{192,0},{1,65},{65,129},{129,193},{193,1... | collective-permute-start | bytes 589832 | tf_op jit(solution)/shard_map/ppermute | solution.py:325
  79.4 7.7 %collective-permute-start.22 = (f32[6,32,256]{2,1,0:T(8,128)S(1)}, f32[6,32,256]{2,1,0:T(8,128)S(1)}, u32[]{:S(2)}, u32[]{:S(2)}) collective-permute-start(f32[6,32,256]{2,1,0:T(8,128)S(1)} %add_select_fusion), channel_id=1, source_target_pairs={{0,128},{64,192},{128,0},{192,64},{1,129},{65,193},{129,1},{193,65... | collective-permute-start | bytes 589832 | tf_op jit(solution)/shard_map/ppermute | solution.py:325
  80.6 7.1 %collective-permute-start.23 = (f32[6,32,256]{2,1,0:T(8,128)S(1)}, f32[6,32,256]{2,1,0:T(8,128)S(1)}, u32[]{:S(2)}, u32[]{:S(2)}) collective-permute-start(f32[6,32,256]{2,1,0:T(8,128)S(1)} %add_select_fusion), channel_id=1, source_target_pairs={{0,192},{64,0},{128,64},{192,128},{1,193},{65,1},{129,65},{193,129... | collective-permute-start | bytes 589832 | tf_op jit(solution)/shard_map/ppermute | solution.py:325
  82.6 16.6 %collective-permute-start.24 = (f32[256,512]{1,0:T(8,128)S(1)}, f32[256,512]{1,0:T(8,128)}, u32[]{:S(2)}, u32[]{:S(2)}) collective-permute-start(f32[256,512]{1,0:T(8,128)S(1)} %collective-permute-done.16), channel_id=1, source_target_pairs={{64,128},{65,129},{66,130},{67,131},{68,132},{69,133},{70,134},{71... | collective-permute-start | bytes 1572872 | tf_op jit(solution)/shard_map/ppermute | solution.py:255
  100.4 4.7 %collective-permute-start.27 = (f32[256,512]{1,0:T(8,128)S(1)}, f32[256,512]{1,0:T(8,128)S(1)}, u32[]{:S(2)}, u32[]{:S(2)}) collective-permute-start(f32[256,512]{1,0:T(8,128)S(1)} %get-tuple-element.32), channel_id=1, source_target_pairs={{0,32},{1,33},{2,34},{3,35},{4,36},{5,37},{6,38},{7,39},{8,40},{9,... | collective-permute-start | bytes 1572872 | tf_op jit(solution)/shard_map/ppermute | solution.py:360
  101.7 4.1 %collective-permute-start.26 = (f32[256,512]{1,0:T(8,128)S(1)}, f32[256,512]{1,0:T(8,128)S(1)}, u32[]{:S(2)}, u32[]{:S(2)}) collective-permute-start(f32[256,512]{1,0:T(8,128)S(1)} %get-tuple-element.31), channel_id=1, source_target_pairs={{0,32},{32,0},{1,33},{33,1},{2,34},{34,2},{3,35},{35,3},{4,36},{36... | collective-permute-start | bytes 1572872 | tf_op jit(solution)/shard_map/ppermute | solution.py:359
  103.9 3.1 %collective-permute-start.25 = (f32[4,6,32,256]{3,2,1,0:T(8,128)S(1)}, f32[4,6,32,256]{3,2,1,0:T(8,128)S(1)}, u32[]{:S(2)}, u32[]{:S(2)}) collective-permute-start(f32[4,6,32,256]{3,2,1,0:T(8,128)S(1)} %pad_maximum_fusion.3), channel_id=1, source_target_pairs={{0,32},{32,0},{1,33},{33,1},{2,34},{34,2},{3,35},{35,3},{4,36},{36... | collective-permute-start | bytes 2359304 | tf_op jit(solution)/shard_map/ppermute | solution.py:332
Sparse Core Ops, SparseCore 0:
  38.4 89.4 all-gather.2
